TPU v7x, 32 devices: a whole 2x2x4 slice. The times are simulated.
32 devices in a mesh: batch: 16 (over z, y, core), seq: 2 (over x).
Axes of the slice: x: 2, y: 2, z: 4, core: 2. Of those that a mesh axis runs over, the one named last changes fastest.
Arguments:
- tokens: bfloat16 [48, 1024, 1024], P('batch', 'seq'), may hold values from -6 to 6
- cotangent: bfloat16 [48, 1024, 1024], P('batch', 'seq'), may hold values from -6 to 6
- layout: int32 [4], replicated, may hold values from 0 to 3, each once
- attention_norm_gain: float32 [1024], replicated, may hold values from 0.1 to 1.9
- feedforward_norm_gain: float32 [1024], replicated, may hold values from 0.1 to 1.9
- query_weight: bfloat16 [1024, 1024], P('batch'), may hold values from -0.25 to 0.25
- key_weight: bfloat16 [1024, 1024], P('batch'), may hold values from -0.25 to 0.25
- value_weight: bfloat16 [1024, 1024], P('batch'), may hold values from -0.1875 to 0.1875
- attention_output_weight: bfloat16 [1024, 1024], P('batch'), may hold values from -0.5 to 0.5
- up_weight: bfloat16 [1024, 4096], P('batch'), may hold values from -0.1875 to 0.1875
- down_weight: bfloat16 [4096, 1024], P('batch'), may hold values from -0.09375 to 0.09375
- query_down_adapter: bfloat16 [1024, 4], replicated, may hold values from -0.1875 to 0.1875
- query_up_adapter: bfloat16 [4, 1024], replicated, may hold values from -0.1796875 to 0.1796875
- value_down_adapter: bfloat16 [1024, 4], replicated, may hold values from -0.1875 to 0.1875
- value_up_adapter: bfloat16 [4, 1024], replicated, may hold values from -0.1796875 to 0.1796875
Outputs:
- layer_out: bfloat16 [48, 1024, 1024], P('batch', 'seq')
- input_grad: bfloat16 [48, 1024, 1024], P('batch', 'seq')
- grad_qa: float32 [1024, 4], replicated
- query_up_gradient: float32 [4, 1024], replicated
- grad_va: float32 [1024, 4], replicated
- value_up_gradient: float32 [4, 1024], replicated
Inputs may be any that keep to these rules, and one draw needn't show every extreme that they name: `layout`: a permutation: each position block of a document is held by exactly one stored block, the same for all documents.
All inputs are finite; a program needn't handle non-finite values.
Results may differ from a plain program's by a relative error of at most 0.018.
Values may be sent and summed in bfloat16 or wider, within the bound.
A program may use at most 384 MiB of HBM per device.

v0:
```python
import functools
import math

import jax
import jax.numpy as jnp
from jax import lax
from jax.experimental import pallas as pl
from jax.experimental.pallas import tpu as pltpu
from jax.sharding import PartitionSpec as P


EPSILON = 1e-05
ADAPTER_SCALE = 8.0
SCORE_SCALE = 0.125
NEG_FILL = -1e30
GELU_C = 0.7978845608028654
LOG2E = math.log2(math.e)
F32 = jnp.float32
BF = jnp.bfloat16
NN = (((1,), (0,)), ((), ()))
NT = (((1,), (1,)), ((), ()))
TN = (((0,), (0,)), ((), ()))
AXES = ("batch", "seq")


def dot(a, b, dims=NN):
    return lax.dot_general(a, b, dims, preferred_element_type=F32)


def normalise(x):
    mean = jnp.mean(x, axis=-1, keepdims=True)
    centred = x - mean
    inv = lax.rsqrt(jnp.mean(centred * centred, axis=-1, keepdims=True) + EPSILON)
    return centred * inv, inv


def norm_back(xh, inv, gain, up):
    t = up * gain
    return inv * (t - jnp.mean(t, axis=-1, keepdims=True) - xh * jnp.mean(t * xh, axis=-1, keepdims=True))


def gelu_parts(u):
    cubic = 0.044715 * u * u
    th = jnp.tanh(GELU_C * (u + cubic * u))
    half = 0.5 * (1.0 + th)
    return half * u, half + (0.5 * GELU_C) * u * (1.0 - th * th) * (1.0 + 3.0 * cubic)


MESH = pl.DeviceIdType.MESH


def flip(i, bits, width=5):
    out = 0
    for n in range(width):
        bit = 1 << n
        out = out + ((i // bit) % 2 + (bits // bit) % 2) % 2 * bit
    return out


def trade(b, s):
    return b - b % 2 + s % 2, s - s % 2 + b % 2


class Place:
    def __init__(self, nb, ns):
        self.nb, self.ns = nb, ns
        self.b, self.s = lax.axis_index("batch"), lax.axis_index("seq")
        self.lines = nb // 4
        self.line = self.b // 4
        self.partner = trade(self.b, self.s)
        self.stays = self.b % 2 == self.s % 2
        self.doc, self.part = trade(self.b, self.s)

    def peer(self, r):
        return trade(self.doc, flip(self.part, r))

    def greet(self, ways):
        bar = pltpu.get_barrier_semaphore()
        for device, cond in ways:
            def hello(device=device):
                pl.semaphore_signal(bar, inc=1, device_id=device, device_id_type=MESH)
            hello() if cond is None else pl.when(cond)(hello)
        count = 0
        for _, cond in ways:
            count = count + (1 if cond is None else jnp.where(cond, 1, 0))
        pl.semaphore_wait(bar, count)

    def gather_ways(self):
        b, s = self.b, self.s
        return [((b + 4, s), self.line + 1 < self.lines), ((b - 4, s), self.line > 0),
                ((flip(b, 2), s), None), ((flip(b, 1), s), None)]


class Gather:
    def __init__(self, place, own, full, send, recv):
        self.p, self.own, self.full, self.send, self.recv = place, own, full, send, recv

    def part(self, line, pair=0, core=0):
        b = self.p.b
        return line * 4 + (b // 2 + pair) % 2 * 2 + (b + core) % 2

    def copy(self, i, way, src=None):
        p = self.p
        to = [p.b + 4, p.b - 4, self.part(p.line, 1), self.part(p.line, 0, 1)][way]
        return pltpu.make_async_remote_copy(
            src_ref=self.full.at[i] if src is None else src, dst_ref=self.full.at[i],
            send_sem=self.send.at[way, i], recv_sem=self.recv.at[i],
            device_id=(to, p.s), device_id_type=MESH)

    def mine(self):
        return pltpu.make_async_copy(self.own, self.full.at[self.p.b], self.recv.at[self.p.b])

    def start(self):
        p = self.p
        pl.when(p.line + 1 < p.lines)(lambda: self.copy(p.b, 0, self.own).start())
        pl.when(p.line > 0)(lambda: self.copy(p.b, 1, self.own).start())
        self.copy(p.b, 2, self.own).start()
        self.copy(p.b, 3, self.own).start()
        self.mine().start()

    def hop(self, k, pairs=True):
        p = self.p

        def take(way, line):
            i = self.part(line)
            self.copy(i, way).wait_recv()
            more = p.line + 1 < p.lines if way == 0 else p.line > 0
            pl.when(more)(lambda: self.copy(i, way).start())
            if pairs:
                self.copy(i, 2).start()
            self.copy(i, 3).start()

        below, above = p.line - k, p.line + k
        pl.when(below >= 0)(lambda: take(0, below))
        pl.when(above < p.lines)(lambda: take(1, above))

    def pair_line(self, line):
        self.copy(self.part(line), 2).start()

    def relay_line(self, line):
        i = self.part(line, 1)
        self.copy(i, 2).wait_recv()
        self.copy(i, 3).start()

    def relay(self, k):
        p = self.p
        if k == 0:
            self.relay_line(p.line)
        else:
            pl.when(p.line >= k)(lambda: self.relay_line(p.line - k))
            pl.when(p.line + k < p.lines)(lambda: self.relay_line(p.line + k))

    def from_core(self, line, pair):
        self.copy(self.part(line, pair, 1), 3).wait_recv()

    def finish(self):
        self.mine().wait()
        for line in range(self.p.lines):
            for pair in range(2):
                self.from_core(line, pair)

    def drain(self):
        p = self.p
        for line in range(p.lines):
            i = self.part(line)
            pl.when((p.line >= line) & (p.line + 1 < p.lines))(lambda i=i: self.copy(i, 0).wait_send())
            pl.when((p.line <= line) & (p.line > 0))(lambda i=i: self.copy(i, 1).wait_send())
            self.copy(i, 2).wait_send()
            self.copy(i, 3).wait_send()
            self.copy(self.part(line, 1), 3).wait_send()

    def steps(self):
        out = [self.start]
        for k in range(1, self.p.lines):
            out.append(functools.partial(run, [functools.partial(self.hop, k), functools.partial(self.relay, k - 1)]))
        out.append(functools.partial(self.relay, self.p.lines - 1))
        out.append(self.finish)
        return out


def run(calls):
    for call in calls:
        call()


def project_kernel(nb, ns, x_hbm, wq_ref, wk_ref, wv_ref, wo_ref, gain_ref, down_ref, ups_ref,
                   q_out, k_out, v_out, low_out, x_out, wq_out, wk_out, wv_out, wo_out,
                   xs, n1s, stage, lows, ws, send, recv, xsend, xrecv, osend, orecv, local_sem):
    docs, rows, d = x_hbm.shape
    w = d // ns
    p = Place(nb, ns)
    others = [p.peer(r) for r in range(1, ns)]
    p.greet(p.gather_ways() + [(p.partner, jnp.logical_not(p.stays))] + [(o, None) for o in others])

    def x_remote(i):
        return pltpu.make_async_remote_copy(
            src_ref=x_hbm.at[i], dst_ref=xs.at[i], send_sem=xsend.at[i], recv_sem=xrecv.at[i],
            device_id=p.partner, device_id_type=MESH)

    def x_local(i):
        return pltpu.make_async_copy(x_hbm.at[i], xs.at[i], xrecv.at[i])

    def x_keep(i):
        return pltpu.make_async_copy(xs.at[i], x_out.at[i], local_sem.at[i])

    for i in range(docs):
        pl.when(p.stays)(lambda i=i: x_local(i).start())
        pl.when(jnp.logical_not(p.stays))(lambda i=i: x_remote(i).start())

    def first(i):
        pl.when(p.stays)(lambda: x_local(i).wait())
        pl.when(jnp.logical_not(p.stays))(lambda: x_remote(i).wait())
        x_keep(i).start()
        xh, _ = normalise(xs[i].astype(F32))
        n1 = (xh * gain_ref[...]).astype(BF)
        n1s[i] = n1
        lows[i] = dot(n1, down_ref[...]).astype(BF)

    outs = (q_out, k_out, v_out)

    def away(part, i, r):
        return pltpu.make_async_remote_copy(
            src_ref=stage.at[part, i, flip(p.part, r)], dst_ref=outs[part].at[p.part, i],
            send_sem=osend.at[part, i, r], recv_sem=orecv.at[part, i, r],
            device_id=p.peer(r), device_id_type=MESH)

    def home(part, i):
        return pltpu.make_async_copy(stage.at[part, i, p.part], outs[part].at[p.part, i], osend.at[part, i, 0])

    def product(part, i):
        y = dot(n1s[i], ws[part].reshape(d, d)) + dot(lows[i], ups_ref[part])
        y = y.astype(BF)
        for g in range(ns):
            stage[part, i, g] = y[:, g * w:(g + 1) * w]
        for n in range(3):
            @pl.when(part == n)
            def _():
                home(n, i).start()
                for r in range(1, ns):
                    away(n, i, r).start()

    gathers = [Gather(p, own, full, send.at[n], recv.at[n]) for n, (own, full) in enumerate(
        ((wq_ref, ws.at[0]), (wk_ref, ws.at[1]), (wv_ref, ws.at[2]), (wo_ref, ws.at[3])))]
    keeps = [pltpu.make_async_copy(ws.at[n], out, local_sem.at[docs + n])
             for n, out in enumerate((wq_out, wk_out, wv_out, wo_out))]
    low_keep = pltpu.make_async_copy(lows, low_out, local_sem.at[docs + 4])

    lists = [g.steps() for g in gathers]
    delays = (0, 0, 2, 4)
    ready = [len(lists[0]) - 1 + delay for delay in delays]

    def slot(t):
        for n, steps in enumerate(lists):
            if 0 <= t - delays[n] < len(steps):
                steps[t - delays[n]]()
            if t == ready[n]:
                keeps[n].start()

    for t in range(ready[0] + 1):
        slot(t)
    places = {2 * docs - 5 + 2 * n: t for n, t in enumerate(range(ready[0] + 1, ready[3] + 1))}

    def one_product(n, carry):
        early = n < 2 * docs
        part = jnp.where(early, n % 2, 2)
        i = jnp.where(early, n // 2, n - 2 * docs)
        pl.when(early & (part == 0))(lambda: first(i))
        product(part, i)
        for at, t in places.items():
            pl.when(n == at)(functools.partial(slot, t))
        return carry

    lax.fori_loop(0, 3 * docs, one_product, 0)
    low_keep.start()
    for part in range(3):
        for i in range(docs):
            home(part, i).wait()
            for r in range(1, ns):
                away(part, i, r).wait()
    for i in range(docs):
        x_keep(i).wait()
    for keep in keeps:
        keep.wait()
    low_keep.wait()
    for g in gathers:
        g.drain()


def project(nb, ns, x, wq, wk, wv, wo, gain, down, ups):
    docs, rows, d = x.shape
    w = d // ns
    any_spec = pl.BlockSpec(memory_space=pl.ANY)
    vmem = pl.BlockSpec(memory_space=pltpu.VMEM)
    head = jax.ShapeDtypeStruct((ns, docs, rows, w), BF)
    full = jax.ShapeDtypeStruct((nb,) + wq.shape, BF)
    dma = pltpu.SemaphoreType.DMA
    return pl.pallas_call(
        functools.partial(project_kernel, nb, ns),
        in_specs=[any_spec] * 5 + [vmem] * 3,
        out_specs=[any_spec] * 9,
        out_shape=[head] * 3 + [jax.ShapeDtypeStruct((docs, rows, 128), BF), jax.ShapeDtypeStruct(x.shape, BF)] + [full] * 4,
        scratch_shapes=[pltpu.VMEM(x.shape, BF), pltpu.VMEM(x.shape, BF), pltpu.VMEM((3, docs, ns, rows, w), BF),
                        pltpu.VMEM((docs, rows, 128), BF)] + [pltpu.VMEM((4,) + full.shape, BF)] + [
                        dma((4, 4, nb)), dma((4, nb)), dma((docs,)), dma((docs,)),
                        dma((3, docs, ns)), dma((3, docs, ns)), dma((docs + 5,))],
        compiler_params=pltpu.CompilerParams(collective_id=0, has_side_effects=True, vmem_limit_bytes=60 << 20),
        name="projections",
    )(x, wq, wk, wv, wo, gain, down, ups)


def in_order(ref, where, blocks, size):
    per = ref.shape[2] // size
    out = []
    for p in range(blocks):
        s = where[p]
        out.append(ref[s // per, 0, pl.ds(pl.multiple_of((s % per) * size, size), size), :])
    return jnp.concatenate(out, axis=0)


def chosen(blocks, which):
    out = blocks[0]
    for t in range(1, len(blocks)):
        out = jnp.where(which == t, blocks[t], out)
    return out


def picked(ref, where, blocks, size):
    per = ref.shape[2] // size
    stored = [ref[t // per, 0, (t % per) * size:(t % per + 1) * size, :] for t in range(blocks)]
    return jnp.concatenate([chosen(stored, where[p]) for p in range(blocks)], axis=0)


def store_back(ref, value, where, blocks, size):
    per = ref.shape[2] // size
    for t in range(blocks):
        piece = value[:size]
        for p in range(1, blocks):
            piece = jnp.where(where[p] == t, value[p * size:(p + 1) * size], piece)
        ref[t // per, 0, (t % per) * size:(t % per + 1) * size, :] = piece


PACE = 4


def attention_forward_kernel(nb, ns, size, tile, where, q_ref, k_ref, v_ref, cot_hbm, up_hbm,
                             o_ref, lse_ref, cot_out, up_out, own, send, recv, csend, crecv, own_sem):
    docs = cot_hbm.shape[0]
    p = Place(nb, ns)
    step = pl.program_id(0) * pl.num_programs(1) + pl.program_id(1)
    steps = docs * (up_hbm.shape[0] * nb // ns // 128)
    gather = Gather(p, own, up_out, send, recv)
    events = gather.steps()

    def cross(i):
        return pltpu.make_async_remote_copy(
            src_ref=cot_hbm.at[i], dst_ref=cot_out.at[i], send_sem=csend.at[i], recv_sem=crecv.at[i],
            device_id=p.partner, device_id_type=MESH)

    def begin():
        fetch = pltpu.make_async_copy(up_hbm, own, own_sem)
        fetch.start()
        p.greet(p.gather_ways() + [(p.partner, jnp.logical_not(p.stays))])
        fetch.wait()
        events[0]()
        for i in range(docs):
            pl.when(jnp.logical_not(p.stays))(lambda i=i: cross(i).start())

    def end():
        for n, event in enumerate(events):
            if n and PACE * n >= steps:
                event()
        for i in range(docs):
            pl.when(jnp.logical_not(p.stays))(lambda i=i: cross(i).wait())
        gather.drain()

    pl.when(step == 0)(begin)
    for n, event in enumerate(events):
        if n and PACE * n < steps:
            pl.when(step == PACE * n)(event)

    lane = lax.broadcasted_iota(jnp.int32, (1, 128), 1)
    parts, rows = q_ref.shape[0], q_ref.shape[2]
    n = parts * rows
    blocks = n // size
    q = picked(q_ref, where, blocks, size)
    k = picked(k_ref, where, blocks, size)
    v = picked(v_ref, where, blocks, size)
    vt = v.T
    c = SCORE_SCALE * LOG2E
    tri = lax.broadcasted_iota(jnp.int32, (tile, tile), 0) <= lax.broadcasted_iota(jnp.int32, (tile, tile), 1)
    work = [(i, h) for i in range(n // tile) for h in range(2)]
    lses = [[], []]
    mixed = {}

    def scores(i, h):
        qm = jnp.where((lane < 64) == (h == 0), q[i * tile:(i + 1) * tile], jnp.zeros((), BF))
        return dot(k[:(i + 1) * tile], qm, NT)

    ahead = scores(*work[0])
    for t, (i, h) in enumerate(work):
        st = ahead
        if t + 1 < len(work):
            ahead = scores(*work[t + 1])
        kk = (i + 1) * tile
        diag = jnp.where(tri, st[i * tile:], NEG_FILL)
        st = diag if i == 0 else jnp.concatenate([st[: i * tile], diag], axis=0)
        m = jnp.max(st, axis=0, keepdims=True) * c
        e = jnp.exp2(st * c - m)
        l = jnp.sum(e, axis=0, keepdims=True)
        o = dot(vt[64 * h:64 * h + 64, :kk], e.astype(BF))
        mixed[i, h] = o * (1.0 / l)
        lses[h].append(m + jnp.log2(l))
    outs = [jnp.concatenate([mixed[i, 0], mixed[i, 1]], axis=0).T.astype(BF) for i in range(n // tile)]
    store_back(o_ref, jnp.concatenate(outs, axis=0), where, blocks, size)
    for h in range(2):
        lse_ref[0, 0, h:h + 1, :] = jnp.concatenate(lses[h], axis=1)

    pl.when(step == steps - 1)(end)


def attention_forward(nb, ns, where, q, k, v, cot, up, size, tile=256):
    parts, docs, rows, w = q.shape
    pairs = w // 128
    n = parts * rows
    spec = pl.BlockSpec((parts, 1, rows, 128), lambda d, p: (0, d, 0, p))
    any_spec = pl.BlockSpec(memory_space=pl.ANY)
    dma = pltpu.SemaphoreType.DMA
    return pl.pallas_call(
        functools.partial(attention_forward_kernel, nb, ns, size, tile),
        grid=(docs, pairs),
        in_specs=[pl.BlockSpec(memory_space=pltpu.SMEM), spec, spec, spec] + [any_spec] * 2,
        out_specs=[spec, pl.BlockSpec((1, 1, 2, n), lambda d, p: (d, p, 0, 0))] + [any_spec] * 2,
        out_shape=[jax.ShapeDtypeStruct((parts, docs, rows, w), BF),
                   jax.ShapeDtypeStruct((docs, pairs, 2, n), F32),
                   jax.ShapeDtypeStruct(cot.shape, BF),
                   jax.ShapeDtypeStruct((nb,) + up.shape, BF)],
        scratch_shapes=[pltpu.VMEM(up.shape, BF), dma((4, nb)), dma((nb,)), dma((docs,)), dma((docs,)), dma],
        compiler_params=pltpu.CompilerParams(collective_id=1, has_side_effects=True, vmem_limit_bytes=60 << 20),
        name="attention_forward",
    )(where, q, k, v, cot, up)


def attention_backward_kernel(size, tile, where, q_ref, k_ref, v_ref, o_ref, g_ref, lse_ref, dq_ref, dk_ref, dv_ref, dqt):
    parts, rows = q_ref.shape[0], q_ref.shape[2]
    n = parts * rows
    blocks = n // size
    q = in_order(q_ref, where, blocks, size)
    k = in_order(k_ref, where, blocks, size)
    v = in_order(v_ref, where, blocks, size)
    o = in_order(o_ref, where, blocks, size)
    g = in_order(g_ref, where, blocks, size)
    kt = k.T
    lane = lax.broadcasted_iota(jnp.int32, (1, 128), 1)
    c = SCORE_SCALE * LOG2E
    tri = lax.broadcasted_iota(jnp.int32, (tile, tile), 0) <= lax.broadcasted_iota(jnp.int32, (tile, tile), 1)
    prod = (o.astype(F32) * g.astype(F32)).astype(BF)
    heads = (lax.broadcasted_iota(jnp.int32, (8, 128), 1) // 64 == lax.broadcasted_iota(jnp.int32, (8, 128), 0)).astype(BF)
    delta = dot(heads, prod, NT)
    zero = jnp.zeros((), BF)
    masks = [(lane < 64) == (h == 0) for h in range(2)]
    qms = [jnp.where(mk, q, zero) for mk in masks]
    gms = [jnp.where(mk, g, zero) for mk in masks]
    lse = lse_ref[0, 0]
    dks, dvs = [], []
    work = [(j, h) for j in range(n // tile) for h in range(2)]

    def products(j, h):
        lo, hi = j * tile, (j + 1) * tile
        return dot(k[lo:hi], qms[h][lo:], NT), dot(v[lo:hi], gms[h][lo:], NT)

    ahead = products(*work[0])
    for t, (j, h) in enumerate(work):
        st, dp = ahead
        if t + 1 < len(work):
            ahead = products(*work[t + 1])
        lo, hi = j * tile, (j + 1) * tile
        p = jnp.exp2(st * c - lse[h:h + 1, lo:])
        diag = jnp.where(tri, p[:, :tile], 0.0)
        p = diag if hi == n else jnp.concatenate([diag, p[:, tile:]], axis=1)
        ds = (p * (dp - delta[h:h + 1, lo:])).astype(BF)
        dvh = dot(p.astype(BF), gms[h][lo:])
        dkh = dot(ds, qms[h][lo:])
        dv = dvh if h == 0 else dv + dvh
        dk = dkh if h == 0 else dk + dkh
        dqh = dot(kt[64 * h:64 * h + 64, lo:hi], ds)
        if j == 0:
            dqt[64 * h:64 * h + 64, :] = dqh
        else:
            dqt[64 * h:64 * h + 64, lo:] += dqh
        if h == 1:
            dks.append((dk * SCORE_SCALE).astype(BF))
            dvs.append(dv.astype(BF))
    store_back(dq_ref, (dqt[...] * SCORE_SCALE).T.astype(BF), where, blocks, size)
    store_back(dk_ref, jnp.concatenate(dks, axis=0), where, blocks, size)
    store_back(dv_ref, jnp.concatenate(dvs, axis=0), where, blocks, size)


def attention_backward(where, q, k, v, o, g, lse, size, tile=256):
    parts, docs, rows, w = q.shape
    pairs = w // 128
    n = parts * rows
    spec = pl.BlockSpec((parts, 1, rows, 128), lambda d, p: (0, d, 0, p))
    return pl.pallas_call(
        functools.partial(attention_backward_kernel, size, tile),
        grid=(docs, pairs),
        in_specs=[pl.BlockSpec(memory_space=pltpu.SMEM)] + [spec] * 5
        + [pl.BlockSpec((1, 1, 2, n), lambda d, p: (d, p, 0, 0))],
        out_specs=[spec] * 3,
        out_shape=[jax.ShapeDtypeStruct(q.shape, BF)] * 3,
        scratch_shapes=[pltpu.VMEM((128, n), F32)],
        compiler_params=pltpu.CompilerParams(vmem_limit_bytes=60 << 20),
        name="attention_backward",
    )(where, q, k, v, o, g, lse)


def middle_kernel(nb, ns, x_hbm, att_hbm, kept_hbm, cot_hbm, gain_ref, wo_hbm, up_hbm, down_hbm,
                  out_hbm, rg_hbm, mix_hbm,
                  xs, atts, cots, wos, downs, ups, acc, xhs, dn, n2s, invs, us, gs,
                  send, recv, asend, arecv, msend, mrecv, load, store):
    docs, rows, d = x_hbm.shape
    w = d // ns
    p = Place(nb, ns)
    held = down_hbm.shape[0]
    chunk = 2 * held
    loads = [pltpu.make_async_copy(wo_hbm, wos, load.at[0])]
    for i in range(docs):
        loads.append(pltpu.make_async_copy(x_hbm.at[i], xs.at[i], load.at[1 + i]))
    loads.append(pltpu.make_async_copy(up_hbm, ups, load.at[1 + docs]))
    for copy in loads:
        copy.start()

    def cot_load(source):
        return pltpu.make_async_copy(source, cots, load.at[2 + docs])

    pl.when(p.stays)(lambda: cot_load(kept_hbm).start())
    pl.when(jnp.logical_not(p.stays))(lambda: cot_load(cot_hbm).start())
    p.greet(p.gather_ways() + [(p.peer(r), None) for r in range(1, ns)])

    gather = Gather(p, down_hbm, downs, send, recv)

    def att_away(i, r):
        return pltpu.make_async_remote_copy(
            src_ref=att_hbm.at[flip(p.part, r), i], dst_ref=atts.at[p.part, i], send_sem=asend.at[i, r],
            recv_sem=arecv.at[i, r], device_id=p.peer(r), device_id_type=MESH)

    def att_home(i):
        return pltpu.make_async_copy(att_hbm.at[p.part, i], atts.at[p.part, i], arecv.at[i, 0])

    for i in range(docs):
        att_home(i).start()
        for r in range(1, ns):
            att_away(i, r).start()
    gather.start()
    for copy in loads[:-1]:
        copy.wait()
    for i in range(docs):
        att_home(i).wait()
        for r in range(1, ns):
            att_away(i, r).wait()

    def rows_of(i):
        return pl.ds(pl.multiple_of(i * rows, rows), rows)

    def second_norm(i, carry):
        at = rows_of(i)
        res = xs[i].astype(F32)
        for g in range(ns):
            res = res + dot(atts[g, i], wos[g * w:(g + 1) * w, :])
        acc[at, :] = res
        xh, inv = normalise(res)
        xhs[at, :] = xh
        invs[at, :] = jnp.broadcast_to(inv, (rows, 128))
        n2s[at, :] = (xh * gain_ref[...]).astype(BF)
        dn[at, :] = jnp.zeros((rows, d), F32)
        return carry

    lax.fori_loop(0, docs, second_norm, 0)
    loads[-1].wait()
    cot_load(cot_hbm).wait()
    gather.mine().wait()
    pair = p.b // 2 % 2

    def weights(f):
        base = flip(p.line, f // 2) * 4 + (pair + f) % 2 * 2
        up = ups[:, :, pl.ds(pl.multiple_of(base * held, chunk), chunk)].reshape(d, chunk)
        return up, downs[pl.ds(base, 2)].reshape(chunk, d)

    def hidden(t):
        up, down = weights(t // docs)
        us[t % 2] = dot(n2s[rows_of(t % docs), :], up)
        gs[t % 2] = dot(cots[t % docs], down, NT)

    def one_tile(t, carry):
        f, i = t // docs, t % docs

        @pl.when(t + 1 < nb // 2 * docs)
        def _():
            after = (t + 1) // docs
            pl.when(i == docs - 1)(lambda: gather.from_core(flip(p.line, after // 2), after % 2))

            @pl.when((i == docs - 1) & (f % 2 == 0))
            def _():
                pl.when(f // 2 + 1 < p.lines)(lambda: gather.hop(f // 2 + 1, pairs=False))
                pl.when(f // 2 + 1 < p.lines)(lambda: gather.pair_line(flip(p.line, f // 2 + 1)))

            pl.when((i == min(1, docs - 1)) & (f % 2 == 0))(lambda: gather.relay_line(flip(p.line, f // 2)))

        hidden(jnp.minimum(t + 1, nb // 2 * docs - 1))
        up, down = weights(f)
        act, slope = gelu_parts(us[t % 2])
        pg = (slope * gs[t % 2]).astype(BF)
        at = rows_of(i)
        acc[at, :] += dot(act.astype(BF), down)
        dn[at, :] += dot(pg, up, NT)
        return carry

    gather.from_core(p.line, 0)
    hidden(0)
    lax.fori_loop(0, nb // 2 * docs, one_tile, 0)

    def out_and_grad(i, carry):
        at = rows_of(i)
        xs[i] = acc[at, :].astype(BF)
        rg = cots[i].astype(F32) + norm_back(xhs[at, :], invs[at, :1], gain_ref[...], dn[at, :])
        xhs[at, :] = rg
        mix = dot(rg.astype(BF), wos[...], NT).astype(BF)
        for g in range(ns):
            atts[g, i] = mix[:, g * w:(g + 1) * w]
        for copy in results(i):
            copy.start()
        return carry

    def results(i):
        out = [pltpu.make_async_copy(atts.at[p.part, i], mix_hbm.at[p.part, i], store.at[2, i]),
               pltpu.make_async_copy(xs.at[i], out_hbm.at[i], store.at[0, i]),
               pltpu.make_async_copy(xhs.at[rows_of(i)], rg_hbm.at[i], store.at[1, i])]
        for r in range(1, ns):
            out.append(pltpu.make_async_remote_copy(
                src_ref=atts.at[flip(p.part, r), i], dst_ref=mix_hbm.at[p.part, i], send_sem=msend.at[i, r],
                recv_sem=mrecv.at[i, r], device_id=p.peer(r), device_id_type=MESH))
        return out

    lax.fori_loop(0, docs, out_and_grad, 0)
    for i in range(docs):
        for copy in results(i):
            copy.wait()
    gather.drain()


def middle(nb, ns, x, att, kept, cot, gain, wo, up, down):
    docs, rows, d = x.shape
    w = d // ns
    n = docs * rows
    any_spec = pl.BlockSpec(memory_space=pl.ANY)
    vmem = pl.BlockSpec(memory_space=pltpu.VMEM)
    dma = pltpu.SemaphoreType.DMA
    return pl.pallas_call(
        functools.partial(middle_kernel, nb, ns),
        in_specs=[any_spec] * 4 + [vmem] + [any_spec] * 3,
        out_specs=[any_spec] * 3,
        out_shape=[jax.ShapeDtypeStruct((docs, rows, d), BF), jax.ShapeDtypeStruct((docs, rows, d), F32),
                   jax.ShapeDtypeStruct((ns, docs, rows, w), BF)],
        scratch_shapes=[pltpu.VMEM((docs, rows, d), BF), pltpu.VMEM((ns, docs, rows, w), BF),
                        pltpu.VMEM((docs, rows, d), BF), pltpu.VMEM(wo.shape, BF), pltpu.VMEM((nb,) + down.shape, BF),
                        pltpu.VMEM(up.shape, BF), pltpu.VMEM((n, d), F32),
                        pltpu.VMEM((n, d), F32), pltpu.VMEM((n, d), F32), pltpu.VMEM((n, d), BF),
                        pltpu.VMEM((n, 128), F32), pltpu.VMEM((2, rows, 2 * down.shape[0]), F32),
                        pltpu.VMEM((2, rows, 2 * down.shape[0]), F32),
                        dma((4, nb)), dma((nb,)), dma((docs, ns)), dma((docs, ns)),
                        dma((docs, ns)), dma((docs, ns)), dma((3 + docs,)), dma((3, docs))],
        compiler_params=pltpu.CompilerParams(collective_id=2, has_side_effects=True, vmem_limit_bytes=63 << 20),
        name="feed_forward",
    )(x, att, kept, cot, gain, wo, up, down)


def sum_over_devices(p, mine, first, second, total, sends, recvs):
    b, s, nb, ns = p.b, p.s, p.nb, p.ns
    slot, block = b % 16, b - b % 16
    many = nb // 16 * ns
    at = (b // 16) * ns + s

    def scatter(j):
        return pltpu.make_async_remote_copy(
            src_ref=mine.at[flip(slot, j)], dst_ref=first.at[slot], send_sem=sends.at[0, j], recv_sem=recvs.at[0, j],
            device_id=(block + flip(slot, j), s), device_id_type=MESH)

    def share(j):
        to = flip(at, j)
        return pltpu.make_async_remote_copy(
            src_ref=second.at[at], dst_ref=second.at[at], send_sem=sends.at[1, j], recv_sem=recvs.at[1, j],
            device_id=((to // ns) * 16 + slot, to % ns), device_id_type=MESH)

    def spread(j):
        return pltpu.make_async_remote_copy(
            src_ref=total.at[slot], dst_ref=total.at[slot], send_sem=sends.at[2, j], recv_sem=recvs.at[2, j],
            device_id=(block + flip(slot, j), s), device_id_type=MESH)

    for j in range(1, 16):
        scatter(j).start()
    first[slot] = mine[slot]
    for j in range(1, 16):
        scatter(j).wait()
    second[at] = jnp.sum(first[...], axis=0)
    for j in range(1, many):
        share(j).start()
    for j in range(1, many):
        share(j).wait()
    total[slot] = jnp.sum(second[...], axis=0)
    for j in range(1, 16):
        spread(j).start()
    for j in range(1, 16):
        spread(j).wait()


def sum_ways(p):
    b, s, nb, ns = p.b, p.s, p.nb, p.ns
    slot, block = b % 16, b - b % 16
    at = (b // 16) * ns + s
    ways = [((block + flip(slot, j), s), None) for j in range(1, 16)]
    for j in range(1, nb // 16 * ns):
        to = flip(at, j)
        ways.append((((to // ns) * 16 + slot, to % ns), None))
    return ways


def final_kernel(nb, ns, rank, x_hbm, gain_ref, dq_hbm, dk_hbm, dv_hbm, rg_hbm, low_hbm, wq_hbm, wk_hbm, wv_hbm,
                 down_ref, upq_ref, upv_ref, out_hbm, sum_ref,
                 xs, rgs, ds, wqs, wks, wvs, lows, outs, gds, gqs, gvs, mine, first, second,
                 load, dsend, drecv, osend, orecv, ssend, srecv):
    docs, rows, d = x_hbm.shape
    w = d // ns
    p = Place(nb, ns)
    grads = (dq_hbm, dk_hbm, dv_hbm)
    loads = [pltpu.make_async_copy(a, v, load.at[n]) for n, (a, v) in enumerate(
        ((wq_hbm, wqs), (wk_hbm, wks), (wv_hbm, wvs), (low_hbm, lows), (x_hbm, xs), (rg_hbm, rgs)))]

    def home(part, i):
        return pltpu.make_async_copy(grads[part].at[p.part, i], ds.at[part, p.part, i], drecv.at[part, i, 0])

    def away(part, i, r):
        return pltpu.make_async_remote_copy(
            src_ref=grads[part].at[flip(p.part, r), i], dst_ref=ds.at[part, p.part, i], send_sem=dsend.at[part, i, r],
            recv_sem=drecv.at[part, i, r], device_id=p.peer(r), device_id_type=MESH)

    def out_away(i):
        return pltpu.make_async_remote_copy(
            src_ref=outs.at[i], dst_ref=out_hbm.at[i], send_sem=osend.at[i], recv_sem=orecv.at[i],
            device_id=p.partner, device_id_type=MESH)

    def out_home(i):
        return pltpu.make_async_copy(outs.at[i], out_hbm.at[i], orecv.at[i])

    for i in range(docs):
        for part in range(3):
            home(part, i).start()
            if i == 0:
                loads[part].start()
    for copy in loads[3:]:
        copy.start()
    p.greet([(p.peer(r), None) for r in range(1, ns)] + [(p.partner, jnp.logical_not(p.stays))] + sum_ways(p))
    for i in range(docs):
        for part in range(3):
            for r in range(1, ns):
                away(part, i, r).start()
    gds[...] = jnp.zeros_like(gds)
    gqs[...] = jnp.zeros_like(gqs)
    gvs[...] = jnp.zeros_like(gvs)
    for copy in loads[:4]:
        copy.wait()
    def one_document(i, carry):
        fg = lg = None
        for r in range(ns):
            g = flip(p.part, r)
            cols = pl.ds(pl.multiple_of(g * w, w), w)
            for part, (full, up, total) in enumerate(((wqs, upq_ref, gqs), (wks, None, None), (wvs, upv_ref, gvs))):
                home(part, i).wait() if r == 0 else away(part, i, r).wait()
                piece = ds[part, g, i]
                y = dot(piece, full[:, :, cols].reshape(d, w), NT)
                fg = y if fg is None else fg + y
                if up is not None:
                    y = dot(piece, up[:, cols], NT)
                    lg = y if lg is None else lg + y
                    total[:, cols] += dot(lows[i], piece, TN)

        @pl.when(i == 0)
        def _():
            for copy in loads[4:]:
                copy.wait()

        lgb = lg.astype(BF)
        fg = fg + dot(lgb, down_ref[...], NT)
        xh, inv = normalise(xs[i].astype(F32))
        gds[...] += dot(lgb, (xh * gain_ref[...]).astype(BF), TN)
        outs[i] = (rgs[i] + norm_back(xh, inv, gain_ref[...], fg)).astype(BF)
        pl.when(p.stays)(lambda: out_home(i).start())
        pl.when(jnp.logical_not(p.stays))(lambda: out_away(i).start())
        return carry

    lax.fori_loop(0, docs, one_document, 0)
    upper = lax.broadcasted_iota(jnp.int32, (2 * rank, 1), 0) < rank
    both = jnp.where(upper, gqs[:2 * rank, :], gvs[:2 * rank, :]) * ADAPTER_SCALE
    for n in range(8):
        mine[n] = gds[:8, n * 128:(n + 1) * 128]
        mine[8 + n] = both[:, n * 128:(n + 1) * 128]
    sum_over_devices(p, mine, first, second, sum_ref, ssend, srecv)
    for i in range(docs):
        pl.when(p.stays)(lambda i=i: out_home(i).wait())
        pl.when(jnp.logical_not(p.stays))(lambda i=i: out_away(i).wait())


def final(nb, ns, rank, x, gain, dq, dk, dv, rg, low, wq, wk, wv, down, upq, upv):
    docs, rows, d = x.shape
    w = d // ns
    any_spec = pl.BlockSpec(memory_space=pl.ANY)
    vmem = pl.BlockSpec(memory_space=pltpu.VMEM)
    dma = pltpu.SemaphoreType.DMA
    many = max(16, nb // 16 * ns)
    return pl.pallas_call(
        functools.partial(final_kernel, nb, ns, rank),
        in_specs=[any_spec, vmem] + [any_spec] * 8 + [vmem] * 3,
        out_specs=[any_spec, vmem],
        out_shape=[jax.ShapeDtypeStruct(x.shape, BF), jax.ShapeDtypeStruct((16, 8, 128), F32)],
        scratch_shapes=[pltpu.VMEM(x.shape, BF), pltpu.VMEM(x.shape, F32), pltpu.VMEM((3, ns, docs, rows, w), BF),]
        + [pltpu.VMEM(wq.shape, BF)] * 3
        + [pltpu.VMEM(low.shape, BF), pltpu.VMEM(x.shape, BF)] + [pltpu.VMEM((128, d), F32)] * 3
        + [pltpu.VMEM((16, 8, 128), F32), pltpu.VMEM((16, 8, 128), F32), pltpu.VMEM((nb // 16 * ns, 8, 128), F32),
           dma((6,)), dma((3, docs, ns)), dma((3, docs, ns)), dma((docs,)), dma((docs,)), dma((3, many)), dma((3, many))],
        compiler_params=pltpu.CompilerParams(collective_id=3, has_side_effects=True, vmem_limit_bytes=60 << 20),
        name="projection_gradients",
    )(x, gain, dq, dk, dv, rg, low, wq, wk, wv, down, upq, upv)


def local(
    nb, ns,
    tokens, cotangent, layout, attention_norm_gain, feedforward_norm_gain,
    query_weight, key_weight, value_weight, attention_output_weight, up_weight, down_weight,
    query_down_adapter, query_up_adapter, value_down_adapter, value_up_adapter,
):
    docs, rows, d = tokens.shape
    size = rows * ns // layout.shape[0]
    rank = query_up_adapter.shape[0]
    down = jnp.pad(jnp.concatenate([query_down_adapter, value_down_adapter], axis=1), ((0, 0), (0, 128 - 2 * rank)))
    upq = jnp.pad((ADAPTER_SCALE * query_up_adapter).astype(BF), ((0, 128 - rank), (0, 0)))
    upv = jnp.pad((ADAPTER_SCALE * value_up_adapter).astype(BF), ((rank, 128 - 2 * rank), (0, 0)))
    where = jnp.argsort(layout).astype(jnp.int32)
    gain1 = attention_norm_gain[None]
    gain2 = feedforward_norm_gain[None]

    q, k, v, low, x, wq, wk, wv, wo = project(
        nb, ns, tokens, query_weight, key_weight, value_weight, attention_output_weight, gain1, down,
        jnp.stack([upq, jnp.zeros_like(upq), upv]))
    att, lse, cot, w_up = attention_forward(nb, ns, where, q, k, v, cotangent, up_weight, size)
    out, rg, mix = middle(nb, ns, x, att, cotangent, cot, gain2, wo.reshape(d, d), w_up, down_weight)
    swap = []
    for b in range(nb):
        for s in range(ns):
            if b % 2 != s % 2:
                b2, s2 = trade(b, s)
                swap.append((b * ns + s, b2 * ns + s2))
    stays = lax.axis_index("batch") % 2 == lax.axis_index("seq") % 2
    layer_out = jnp.where(stays, out, lax.ppermute(out, AXES, swap))
    dq, dk, dv = attention_backward(where, q, k, v, att, mix, lse, size)
    input_grad, sums = final(nb, ns, rank, x, gain1, dq, dk, dv, rg, low, wq, wk, wv, down, upq, upv)
    sums = sums.reshape(2, d // 128, 2 * rank, 128).transpose(0, 2, 1, 3).reshape(2, 2 * rank, d)
    return (layer_out, input_grad, sums[0, :rank].T, sums[1, :rank], sums[0, rank:].T, sums[1, rank:])


def solution(mesh):
    spec = P("batch", "seq", None)
    weight = P("batch", None)
    return jax.shard_map(
        functools.partial(local, mesh.shape["batch"], mesh.shape["seq"]),
        mesh=mesh,
        in_specs=(spec, spec, P(), P(), P()) + (weight,) * 6 + (P(),) * 4,
        out_specs=(spec, spec, P(), P(), P(), P()),
        check_vma=False,
    )
```

profile of v0, /device:TPU:1, one launch (start us, length us, event | category | flops | bytes accessed | tf_op | source)
XLA Modules:
  0.0 332.0 jit_solution(5830646949193670414)
XLA Ops:
  0.6 0.7 broadcast_multiply_fusion
  1.3 0.7 broadcast_multiply_fusion.1
  2.0 0.7 pad_maximum_fusion.1
  2.8 0.2 copy.23
  2.9 0.9 fusion
  3.9 0.8 pad.12.down_ref
  4.6 0.1 pad.16.clone
  4.7 1.4 sort.17
  6.1 1.0 pad_maximum_fusion.ups_ref
  7.1 67.9 %projections.1 = (bf16[2,3,512,512]{3,2,1,0:T(8,128)(2,1)}, bf16[2,3,512,512]{3,2,1,0:T(8,128)(2,1)}, bf16[2,3,512,512]{3,2,1,0:T(8,128)(2,1)}, bf16[3,512,128]{...) custom-call(bf16[3,512,1024]{2,1,0:T(8,128)(2,1)} %x_hbm.1, ...), custom_call_target="tpu_custom_call" | custom-call | tf_op jit(solution)/shard_map/projections/pallas_call | solution.py:297
  75.0 57.8 %attention_forward.1 = (bf16[2,3,512,512]{3,2,1,0:T(8,128)(2,1)}, f32[3,4,2,1024]{3,2,1,0:T(2,128)}, bf16[3,512,1024]{2,1,0:T(8,128)(2,1)}, bf16[16,64,4096]{2,1,0:T(8,128)(2,1)}) custom-call(s32[4]{0:T(128)} %get-tuple-element.29.where, bf16[2,3,512,512]{3,2,1,0:T(8,128)(2,1)} %get-tuple-element.30.q_ref, bf16[2,3,512,512]{3,2,1,0:T(8,128)(2,1)} %get-tuple-element.31.k_ref, ...), custom_call_target="tpu_custom_call" | custom-call | tf_op jit(solution)/shard_map/attention_forward/pallas_call | solution.py:428
  132.8 85.7 %feed_forward.1 = (bf16[3,512,1024]{2,1,0:T(8,128)(2,1)}, f32[3,512,1024]{2,1,0:T(8,128)}, bf16[2,3,512,512]{3,2,1,0:T(8,128)(2,1)}) custom-call(bf16[3,512,1024]{2,1,0:T(8,128)(2,1)} %get-tuple-element.28.x_hbm, bf16[2,3,512,512]{3,2,1,0:T(8,128)(2,1)} %get-tuple-element.33.att_hbm.o_ref, bf16[3,512,1024]{2,1,0:T(8,128)(2,1)} %kept_hbm.1, ...), custom_call_target="tpu_custom_call" | custom-call | tf_op jit(solution)/shard_map/feed_forward/pallas_call | solution.py:657
  218.6 2.8 collective-permute-start
  221.4 46.9 %attention_backward.1 = (bf16[2,3,512,512]{3,2,1,0:T(8,128)(2,1)}, bf16[2,3,512,512]{3,2,1,0:T(8,128)(2,1)}, bf16[2,3,512,512]{3,2,1,0:T(8,128)(2,1)}) custom-call(s32[4]{0:T(128)} %get-tuple-element.29.where, bf16[2,3,512,512]{3,2,1,0:T(8,128)(2,1)} %get-tuple-element.30.q_ref, bf16[2,3,512,512]{3,2,1,0:T(8,128)(2,1)} %get-tuple-element.31.k_ref, ...), custom_call_target="tpu_custom_call" | custom-call | tf_op jit(solution)/shard_map/attention_backward/pallas_call | solution.py:503
  268.3 0.0 copy-start.1
  268.3 56.5 %projection_gradients.1 = (bf16[3,512,1024]{2,1,0:T(8,128)(2,1)}, f32[16,8,128]{2,1,0:T(8,128)}) custom-call(bf16[3,512,1024]{2,1,0:T(8,128)(2,1)} %get-tuple-element.28.x_hbm, f32[1,1024]{1,0:T(1,128)} %bitcast.28, bf16[2,3,512,512]{3,2,1,0:T(8,128)(2,1)} %get-tuple-element.40.dq_hbm, bf16[2,3,512,512]{3,2,1,0:T(8,128)(2,1)} %get-tuple-element.41.dk_hbm, ...), custom_call_target="tpu_custom_call" | custom-call | tf_op jit(solution)/shard_map/projection_gradients/pallas_call | solution.py:818
  324.8 1.5 slice_bitcast_fusion
  326.3 0.0 copy-start
  326.3 0.0 collective-permute-done
  326.3 0.0 copy-done.1
  326.3 4.0 %broadcast_select_fusion = bf16[3,512,1024]{2,1,0:T(8,128)(2,1)} fusion(bf16[3,512,1024]{2,1,0:T(8,128)(2,1)S(1)} %copy-done.1, bf16[3,512,1024]{2,1,0:T(8,128)(2,1)} %collective-permute-done, pred[]{:T(512)S(6)} %eq.6), kind=kLoop, calls=%fused_computation | loop fusion | flops 1572864 | bytes 9437185 | tf_op jit(solution)/shard_map/jit(_where)/select_n | solution.py:861
  330.3 0.0 copy-done
  330.3 1.7 copy.25
  (1 shorter events, 0.0 us)
Async XLA Ops:
  218.6 107.7 %collective-permute-start = (bf16[3,512,1024]{2,1,0:T(8,128)(2,1)}, bf16[3,512,1024]{2,1,0:T(8,128)(2,1)}, u32[]{:S(2)}, u32[]{:S(2)}) collective-permute-start(bf16[3,512,1024]{2,1,0:T(8,128)(2,1)} %get-tuple-element.37), channel_id=1, source_target_pairs={{1,2},{2,1},{5,6},{6,5},{9,10},{10,9},{13,14},{14,13},{17,18},{18,... | collective-permute-start | bytes 9437192 | tf_op jit(solution)/shard_map/ppermute | solution.py:861
  268.3 58.0 %copy-start.1 = (bf16[3,512,1024]{2,1,0:T(8,128)(2,1)S(1)}, bf16[3,512,1024]{2,1,0:T(8,128)(2,1)}, u32[]{:S(2)}) copy-start(bf16[3,512,1024]{2,1,0:T(8,128)(2,1)} %get-tuple-element.37) | copy-start | bytes 9437188
  326.3 4.1 %copy-start = (bf16[3,512,1024]{2,1,0:T(8,128)(2,1)S(1)}, bf16[3,512,1024]{2,1,0:T(8,128)(2,1)}, u32[]{:S(2)}) copy-start(bf16[3,512,1024]{2,1,0:T(8,128)(2,1)} %get-tuple-element.67) | copy-start | bytes 9437188
where the time goes:
time: 332 us
  Pallas kernels  315 us (95%)
  other arithmetic  8.58 us (3%)
  local copies, waits for them, and re-layouts  5.08 us (2%)
    pallas_call x1, Pallas kernels, middle(): pl.pallas_call(functools.partial(middle_kernel, nb, ns), in_specs=[any_sp...  85.7 us
    pallas_call x1, Pallas kernels, project(): pl.pallas_call(functools.partial(project_kernel, nb, ns), in_specs=[any_s...  67.9 us
    pallas_call x1, Pallas kernels, attention_forward(): pl.pallas_call(functools.partial(attention_forward_kernel, nb, ns, size,...  57.8 us
    pallas_call x1, Pallas kernels, final(): pl.pallas_call(functools.partial(final_kernel, nb, ns, rank), in_specs=[a...  56.5 us
    pallas_call x1, Pallas kernels, attention_backward(): pl.pallas_call(functools.partial(attention_backward_kernel, size, tile),...  46.9 us
  transfers between devices with their start and end apart: 1, of which 0 were waited for; matrix products, arithmetic and copies ran while one was open for 0% of the time, Pallas kernels for 31%

commit v1 on v0

--- a/solution.py
+++ b/solution.py
@@ -20,7 +20,6 @@
 NN = (((1,), (0,)), ((), ()))
 NT = (((1,), (1,)), ((), ()))
 TN = (((0,), (0,)), ((), ()))
-AXES = ("batch", "seq")
 
 
 def dot(a, b, dims=NN):
@@ -308,41 +307,29 @@
     )(x, wq, wk, wv, wo, gain, down, ups)
 
 
-def in_order(ref, where, blocks, size):
-    per = ref.shape[2] // size
-    out = []
-    for p in range(blocks):
-        s = where[p]
-        out.append(ref[s // per, 0, pl.ds(pl.multiple_of((s % per) * size, size), size), :])
-    return jnp.concatenate(out, axis=0)
-
-
-def chosen(blocks, which):
+def chosen(blocks, tests):
     out = blocks[0]
-    for t in range(1, len(blocks)):
-        out = jnp.where(which == t, blocks[t], out)
+    for block, test in zip(blocks[1:], tests[1:]):
+        out = jnp.where(test, block, out)
     return out
 
 
-def picked(ref, where, blocks, size):
+def picked(ref, layout, blocks, size):
     per = ref.shape[2] // size
     stored = [ref[t // per, 0, (t % per) * size:(t % per + 1) * size, :] for t in range(blocks)]
-    return jnp.concatenate([chosen(stored, where[p]) for p in range(blocks)], axis=0)
-
-
-def store_back(ref, value, where, blocks, size):
-    per = ref.shape[2] // size
+    return jnp.concatenate([chosen(stored, [layout[t] == p for t in range(blocks)]) for p in range(blocks)], axis=0)
+
+
+def put_back(value, layout, blocks, size, store):
+    pieces = [value[p * size:(p + 1) * size] for p in range(blocks)]
     for t in range(blocks):
-        piece = value[:size]
-        for p in range(1, blocks):
-            piece = jnp.where(where[p] == t, value[p * size:(p + 1) * size], piece)
-        ref[t // per, 0, (t % per) * size:(t % per + 1) * size, :] = piece
+        store(t, chosen(pieces, [layout[t] == p for p in range(blocks)]))
 
 
 PACE = 4
 
 
-def attention_forward_kernel(nb, ns, size, tile, where, q_ref, k_ref, v_ref, cot_hbm, up_hbm,
+def attention_forward_kernel(nb, ns, size, tile, layout, q_ref, k_ref, v_ref, cot_hbm, up_hbm,
                              o_ref, lse_ref, cot_out, up_out, own, send, recv, csend, crecv, own_sem):
     docs = cot_hbm.shape[0]
     p = Place(nb, ns)
@@ -382,9 +369,9 @@
     parts, rows = q_ref.shape[0], q_ref.shape[2]
     n = parts * rows
     blocks = n // size
-    q = picked(q_ref, where, blocks, size)
-    k = picked(k_ref, where, blocks, size)
-    v = picked(v_ref, where, blocks, size)
+    q = picked(q_ref, layout, blocks, size)
+    k = picked(k_ref, layout, blocks, size)
+    v = picked(v_ref, layout, blocks, size)
     vt = v.T
     c = SCORE_SCALE * LOG2E
     tri = lax.broadcasted_iota(jnp.int32, (tile, tile), 0) <= lax.broadcasted_iota(jnp.int32, (tile, tile), 1)
@@ -411,14 +398,19 @@
         mixed[i, h] = o * (1.0 / l)
         lses[h].append(m + jnp.log2(l))
     outs = [jnp.concatenate([mixed[i, 0], mixed[i, 1]], axis=0).T.astype(BF) for i in range(n // tile)]
-    store_back(o_ref, jnp.concatenate(outs, axis=0), where, blocks, size)
+    per = rows // size
+
+    def store(t, piece):
+        o_ref[t // per, 0, t % per * size:(t % per + 1) * size, :] = piece
+
+    put_back(jnp.concatenate(outs, axis=0), layout, blocks, size, store)
     for h in range(2):
         lse_ref[0, 0, h:h + 1, :] = jnp.concatenate(lses[h], axis=1)
 
     pl.when(step == steps - 1)(end)
 
 
-def attention_forward(nb, ns, where, q, k, v, cot, up, size, tile=256):
+def attention_forward(nb, ns, layout, q, k, v, cot, up, size, tile=256):
     parts, docs, rows, w = q.shape
     pairs = w // 128
     n = parts * rows
@@ -437,80 +429,7 @@
         scratch_shapes=[pltpu.VMEM(up.shape, BF), dma((4, nb)), dma((nb,)), dma((docs,)), dma((docs,)), dma],
         compiler_params=pltpu.CompilerParams(collective_id=1, has_side_effects=True, vmem_limit_bytes=60 << 20),
         name="attention_forward",
-    )(where, q, k, v, cot, up)
-
-
-def attention_backward_kernel(size, tile, where, q_ref, k_ref, v_ref, o_ref, g_ref, lse_ref, dq_ref, dk_ref, dv_ref, dqt):
-    parts, rows = q_ref.shape[0], q_ref.shape[2]
-    n = parts * rows
-    blocks = n // size
-    q = in_order(q_ref, where, blocks, size)
-    k = in_order(k_ref, where, blocks, size)
-    v = in_order(v_ref, where, blocks, size)
-    o = in_order(o_ref, where, blocks, size)
-    g = in_order(g_ref, where, blocks, size)
-    kt = k.T
-    lane = lax.broadcasted_iota(jnp.int32, (1, 128), 1)
-    c = SCORE_SCALE * LOG2E
-    tri = lax.broadcasted_iota(jnp.int32, (tile, tile), 0) <= lax.broadcasted_iota(jnp.int32, (tile, tile), 1)
-    prod = (o.astype(F32) * g.astype(F32)).astype(BF)
-    heads = (lax.broadcasted_iota(jnp.int32, (8, 128), 1) // 64 == lax.broadcasted_iota(jnp.int32, (8, 128), 0)).astype(BF)
-    delta = dot(heads, prod, NT)
-    zero = jnp.zeros((), BF)
-    masks = [(lane < 64) == (h == 0) for h in range(2)]
-    qms = [jnp.where(mk, q, zero) for mk in masks]
-    gms = [jnp.where(mk, g, zero) for mk in masks]
-    lse = lse_ref[0, 0]
-    dks, dvs = [], []
-    work = [(j, h) for j in range(n // tile) for h in range(2)]
-
-    def products(j, h):
-        lo, hi = j * tile, (j + 1) * tile
-        return dot(k[lo:hi], qms[h][lo:], NT), dot(v[lo:hi], gms[h][lo:], NT)
-
-    ahead = products(*work[0])
-    for t, (j, h) in enumerate(work):
-        st, dp = ahead
-        if t + 1 < len(work):
-            ahead = products(*work[t + 1])
-        lo, hi = j * tile, (j + 1) * tile
-        p = jnp.exp2(st * c - lse[h:h + 1, lo:])
-        diag = jnp.where(tri, p[:, :tile], 0.0)
-        p = diag if hi == n else jnp.concatenate([diag, p[:, tile:]], axis=1)
-        ds = (p * (dp - delta[h:h + 1, lo:])).astype(BF)
-        dvh = dot(p.astype(BF), gms[h][lo:])
-        dkh = dot(ds, qms[h][lo:])
-        dv = dvh if h == 0 else dv + dvh
-        dk = dkh if h == 0 else dk + dkh
-        dqh = dot(kt[64 * h:64 * h + 64, lo:hi], ds)
-        if j == 0:
-            dqt[64 * h:64 * h + 64, :] = dqh
-        else:
-            dqt[64 * h:64 * h + 64, lo:] += dqh
-        if h == 1:
-            dks.append((dk * SCORE_SCALE).astype(BF))
-            dvs.append(dv.astype(BF))
-    store_back(dq_ref, (dqt[...] * SCORE_SCALE).T.astype(BF), where, blocks, size)
-    store_back(dk_ref, jnp.concatenate(dks, axis=0), where, blocks, size)
-    store_back(dv_ref, jnp.concatenate(dvs, axis=0), where, blocks, size)
-
-
-def attention_backward(where, q, k, v, o, g, lse, size, tile=256):
-    parts, docs, rows, w = q.shape
-    pairs = w // 128
-    n = parts * rows
-    spec = pl.BlockSpec((parts, 1, rows, 128), lambda d, p: (0, d, 0, p))
-    return pl.pallas_call(
-        functools.partial(attention_backward_kernel, size, tile),
-        grid=(docs, pairs),
-        in_specs=[pl.BlockSpec(memory_space=pltpu.SMEM)] + [spec] * 5
-        + [pl.BlockSpec((1, 1, 2, n), lambda d, p: (d, p, 0, 0))],
-        out_specs=[spec] * 3,
-        out_shape=[jax.ShapeDtypeStruct(q.shape, BF)] * 3,
-        scratch_shapes=[pltpu.VMEM((128, n), F32)],
-        compiler_params=pltpu.CompilerParams(vmem_limit_bytes=60 << 20),
-        name="attention_backward",
-    )(where, q, k, v, o, g, lse)
+    )(layout, q, k, v, cot, up)
 
 
 def middle_kernel(nb, ns, x_hbm, att_hbm, kept_hbm, cot_hbm, gain_ref, wo_hbm, up_hbm, down_hbm,
@@ -723,111 +642,207 @@
     return ways
 
 
-def final_kernel(nb, ns, rank, x_hbm, gain_ref, dq_hbm, dk_hbm, dv_hbm, rg_hbm, low_hbm, wq_hbm, wk_hbm, wv_hbm,
-                 down_ref, upq_ref, upv_ref, out_hbm, sum_ref,
-                 xs, rgs, ds, wqs, wks, wvs, lows, outs, gds, gqs, gvs, mine, first, second,
-                 load, dsend, drecv, osend, orecv, ssend, srecv):
+CUTS = 2
+
+
+def backward_kernel(nb, ns, rank, size, tile, layout, q_ref, k_ref, v_ref, o_ref, g_ref, lse_ref, top_hbm, x_hbm, gain_ref,
+                    rg_hbm, low_hbm, wq_hbm, wk_hbm, wv_hbm, down_ref, upq_ref, upv_ref, top_out, out_hbm, sum_ref,
+                    dqt, stage, xs, rgs, ds, wqs, wks, wvs, lows, outs, gds, gqs, gvs, mine, first, second, summed,
+                    load, dsend, drecv, osend, orecv, tsend, trecv, ssend, srecv):
     docs, rows, d = x_hbm.shape
     w = d // ns
     p = Place(nb, ns)
-    grads = (dq_hbm, dk_hbm, dv_hbm)
+    doc, pair = pl.program_id(0), pl.program_id(1)
+    pairs = w // 128
     loads = [pltpu.make_async_copy(a, v, load.at[n]) for n, (a, v) in enumerate(
         ((wq_hbm, wqs), (wk_hbm, wks), (wv_hbm, wvs), (low_hbm, lows), (x_hbm, xs), (rg_hbm, rgs)))]
 
-    def home(part, i):
-        return pltpu.make_async_copy(grads[part].at[p.part, i], ds.at[part, p.part, i], drecv.at[part, i, 0])
-
-    def away(part, i, r):
-        return pltpu.make_async_remote_copy(
-            src_ref=grads[part].at[flip(p.part, r), i], dst_ref=ds.at[part, p.part, i], send_sem=dsend.at[part, i, r],
-            recv_sem=drecv.at[part, i, r], device_id=p.peer(r), device_id_type=MESH)
-
-    def out_away(i):
-        return pltpu.make_async_remote_copy(
-            src_ref=outs.at[i], dst_ref=out_hbm.at[i], send_sem=osend.at[i], recv_sem=orecv.at[i],
+    def away(t, i, r):
+        return pltpu.make_async_remote_copy(
+            src_ref=stage.at[i, t, flip(p.part, r)], dst_ref=ds.at[t, p.part, i], send_sem=dsend.at[t, i, r],
+            recv_sem=drecv.at[t, i, r], device_id=p.peer(r), device_id_type=MESH)
+
+    cut = rows // CUTS
+
+    def out_away(i, n):
+        at = pl.ds(pl.multiple_of(n * cut, cut), cut)
+        return pltpu.make_async_remote_copy(
+            src_ref=outs.at[i, at], dst_ref=out_hbm.at[i, at], send_sem=osend.at[i, n], recv_sem=orecv.at[i, n],
             device_id=p.partner, device_id_type=MESH)
 
-    def out_home(i):
-        return pltpu.make_async_copy(outs.at[i], out_hbm.at[i], orecv.at[i])
-
-    for i in range(docs):
-        for part in range(3):
-            home(part, i).start()
-            if i == 0:
-                loads[part].start()
-    for copy in loads[3:]:
-        copy.start()
-    p.greet([(p.peer(r), None) for r in range(1, ns)] + [(p.partner, jnp.logical_not(p.stays))] + sum_ways(p))
-    for i in range(docs):
-        for part in range(3):
-            for r in range(1, ns):
-                away(part, i, r).start()
-    gds[...] = jnp.zeros_like(gds)
-    gqs[...] = jnp.zeros_like(gqs)
-    gvs[...] = jnp.zeros_like(gvs)
-    for copy in loads[:4]:
-        copy.wait()
-    def one_document(i, carry):
-        fg = lg = None
-        for r in range(ns):
-            g = flip(p.part, r)
-            cols = pl.ds(pl.multiple_of(g * w, w), w)
-            for part, (full, up, total) in enumerate(((wqs, upq_ref, gqs), (wks, None, None), (wvs, upv_ref, gvs))):
-                home(part, i).wait() if r == 0 else away(part, i, r).wait()
-                piece = ds[part, g, i]
-                y = dot(piece, full[:, :, cols].reshape(d, w), NT)
-                fg = y if fg is None else fg + y
-                if up is not None:
-                    y = dot(piece, up[:, cols], NT)
-                    lg = y if lg is None else lg + y
-                    total[:, cols] += dot(lows[i], piece, TN)
+    def out_home(i, n):
+        at = pl.ds(pl.multiple_of(n * cut, cut), cut)
+        return pltpu.make_async_copy(outs.at[i, at], out_hbm.at[i, at], orecv.at[i, n])
+
+    def top_away(i):
+        return pltpu.make_async_remote_copy(
+            src_ref=top_hbm.at[i], dst_ref=top_out.at[i], send_sem=tsend.at[i], recv_sem=trecv.at[i],
+            device_id=p.partner, device_id_type=MESH)
+
+    @pl.when((doc == 0) & (pair == 0))
+    def _():
+        for copy in loads:
+            copy.start()
+        p.greet([(p.peer(r), None) for r in range(1, ns)] + [(p.partner, jnp.logical_not(p.stays))] + sum_ways(p))
+        for i in range(docs):
+            pl.when(jnp.logical_not(p.stays))(lambda i=i: top_away(i).start())
+        gds[...] = jnp.zeros_like(gds)
+        gqs[...] = jnp.zeros_like(gqs)
+        gvs[...] = jnp.zeros_like(gvs)
+
+    @pl.when((doc > 0) & (pair == min(1, pairs - 1)))
+    def _():
+        i = doc - 1
 
         @pl.when(i == 0)
         def _():
-            for copy in loads[4:]:
+            for copy in loads:
                 copy.wait()
 
-        lgb = lg.astype(BF)
-        fg = fg + dot(lgb, down_ref[...], NT)
-        xh, inv = normalise(xs[i].astype(F32))
-        gds[...] += dot(lgb, (xh * gain_ref[...]).astype(BF), TN)
-        outs[i] = (rgs[i] + norm_back(xh, inv, gain_ref[...], fg)).astype(BF)
-        pl.when(p.stays)(lambda: out_home(i).start())
-        pl.when(jnp.logical_not(p.stays))(lambda: out_away(i).start())
-        return carry
-
-    lax.fori_loop(0, docs, one_document, 0)
-    upper = lax.broadcasted_iota(jnp.int32, (2 * rank, 1), 0) < rank
-    both = jnp.where(upper, gqs[:2 * rank, :], gvs[:2 * rank, :]) * ADAPTER_SCALE
-    for n in range(8):
-        mine[n] = gds[:8, n * 128:(n + 1) * 128]
-        mine[8 + n] = both[:, n * 128:(n + 1) * 128]
-    sum_over_devices(p, mine, first, second, sum_ref, ssend, srecv)
-    for i in range(docs):
-        pl.when(p.stays)(lambda i=i: out_home(i).wait())
-        pl.when(jnp.logical_not(p.stays))(lambda i=i: out_away(i).wait())
-
-
-def final(nb, ns, rank, x, gain, dq, dk, dv, rg, low, wq, wk, wv, down, upq, upv):
+        for t in range(3):
+            for r in range(1, ns):
+                away(t, i, r).wait()
+
+        def some_rows(n, carry):
+            at = pl.ds(pl.multiple_of(n * cut, cut), cut)
+            low = lows[i, at, :]
+            fg = lg = None
+            for r in range(ns):
+                g = flip(p.part, r)
+                cols = pl.ds(pl.multiple_of(g * w, w), w)
+                for t, (full, up, total) in enumerate(((wqs, upq_ref, gqs), (wks, None, None), (wvs, upv_ref, gvs))):
+                    piece = ds[t, g, i, at, :] if r else stage[i, t, p.part, at, :]
+                    y = dot(piece, full[:, :, cols].reshape(d, w), NT)
+                    fg = y if fg is None else fg + y
+                    if up is not None:
+                        y = dot(piece, up[:, cols], NT)
+                        lg = y if lg is None else lg + y
+                        total[:, cols] += dot(low, piece, TN)
+            lgb = lg.astype(BF)
+            fg = fg + dot(lgb, down_ref[...], NT)
+            xh, inv = normalise(xs[i, at, :].astype(F32))
+            gds[...] += dot(lgb, (xh * gain_ref[...]).astype(BF), TN)
+            outs[i, at, :] = (rgs[i, at, :] + norm_back(xh, inv, gain_ref[...], fg)).astype(BF)
+            pl.when(p.stays)(lambda: out_home(i, n).start())
+            pl.when(jnp.logical_not(p.stays))(lambda: out_away(i, n).start())
+            return carry
+
+        lax.fori_loop(0, CUTS, some_rows, 0)
+
+    @pl.when(doc < docs)
+    def _():
+        attention_gradients(layout, q_ref, k_ref, v_ref, o_ref, g_ref, lse_ref, stage, dqt, doc, pair, size, tile)
+
+        @pl.when(pair == pairs - 1)
+        def _():
+            for t in range(3):
+                for r in range(1, ns):
+                    away(t, doc, r).start()
+
+    @pl.when((doc == docs) & (pair == pairs - 1))
+    def _():
+        upper = lax.broadcasted_iota(jnp.int32, (2 * rank, 1), 0) < rank
+        both = jnp.where(upper, gqs[:2 * rank, :], gvs[:2 * rank, :]) * ADAPTER_SCALE
+        for n in range(8):
+            mine[n] = gds[:8, n * 128:(n + 1) * 128]
+            mine[8 + n] = both[:, n * 128:(n + 1) * 128]
+        sum_over_devices(p, mine, first, second, summed, ssend, srecv)
+        sum_ref[...] = summed[...]
+        for i in range(docs):
+            for n in range(CUTS):
+                pl.when(p.stays)(lambda i=i, n=n: out_home(i, n).wait())
+                pl.when(jnp.logical_not(p.stays))(lambda i=i, n=n: out_away(i, n).wait())
+            pl.when(jnp.logical_not(p.stays))(lambda i=i: top_away(i).wait())
+
+
+def attention_gradients(layout, q_ref, k_ref, v_ref, o_ref, g_ref, lse_ref, stage, dqt, doc, pair, size, tile):
+    parts, rows = q_ref.shape[0], q_ref.shape[2]
+    n = parts * rows
+    blocks, per = n // size, rows // size
+    q = picked(q_ref, layout, blocks, size)
+    k = picked(k_ref, layout, blocks, size)
+    v = picked(v_ref, layout, blocks, size)
+    o = picked(o_ref, layout, blocks, size)
+    g = picked(g_ref, layout, blocks, size)
+    kt = k.T
+    lane = lax.broadcasted_iota(jnp.int32, (1, 128), 1)
+    c = SCORE_SCALE * LOG2E
+    tri = lax.broadcasted_iota(jnp.int32, (tile, tile), 0) <= lax.broadcasted_iota(jnp.int32, (tile, tile), 1)
+    prod = (o.astype(F32) * g.astype(F32)).astype(BF)
+    heads = (lax.broadcasted_iota(jnp.int32, (8, 128), 1) // 64 == lax.broadcasted_iota(jnp.int32, (8, 128), 0)).astype(BF)
+    delta = dot(heads, prod, NT)
+    zero = jnp.zeros((), BF)
+    masks = [(lane < 64) == (h == 0) for h in range(2)]
+    qms = [jnp.where(mk, q, zero) for mk in masks]
+    gms = [jnp.where(mk, g, zero) for mk in masks]
+    lse = lse_ref[0, 0]
+    dks, dvs = [], []
+    work = [(j, h) for j in range(n // tile) for h in range(2)]
+
+    def products(j, h):
+        lo, hi = j * tile, (j + 1) * tile
+        return dot(k[lo:hi], qms[h][lo:], NT), dot(v[lo:hi], gms[h][lo:], NT)
+
+    ahead = products(*work[0])
+    for t, (j, h) in enumerate(work):
+        st, dp = ahead
+        if t + 1 < len(work):
+            ahead = products(*work[t + 1])
+        lo, hi = j * tile, (j + 1) * tile
+        p = jnp.exp2(st * c - lse[h:h + 1, lo:])
+        diag = jnp.where(tri, p[:, :tile], 0.0)
+        p = diag if hi == n else jnp.concatenate([diag, p[:, tile:]], axis=1)
+        ds = (p * (dp - delta[h:h + 1, lo:])).astype(BF)
+        dvh = dot(p.astype(BF), gms[h][lo:])
+        dkh = dot(ds, qms[h][lo:])
+        dv = dvh if h == 0 else dv + dvh
+        dk = dkh if h == 0 else dk + dkh
+        dqh = dot(kt[64 * h:64 * h + 64, lo:hi], ds)
+        if j == 0:
+            dqt[64 * h:64 * h + 64, :] = dqh
+        else:
+            dqt[64 * h:64 * h + 64, lo:] += dqh
+        if h == 1:
+            dks.append((dk * SCORE_SCALE).astype(BF))
+            dvs.append(dv.astype(BF))
+    lanes = pl.ds(pl.multiple_of(pair * 128, 128), 128)
+    for t, value in enumerate(((dqt[...] * SCORE_SCALE).T.astype(BF), jnp.concatenate(dks, axis=0),
+                               jnp.concatenate(dvs, axis=0))):
+        def store(b, piece, t=t):
+            stage[doc, t, b // per, b % per * size:(b % per + 1) * size, lanes] = piece
+        put_back(value, layout, blocks, size, store)
+
+
+def backward(nb, ns, rank, layout, q, k, v, o, g, lse, top, x, gain, rg, low, wq, wk, wv, down, upq, upv, size, tile=256):
     docs, rows, d = x.shape
+    parts = q.shape[0]
     w = d // ns
+    n = parts * rows
     any_spec = pl.BlockSpec(memory_space=pl.ANY)
     vmem = pl.BlockSpec(memory_space=pltpu.VMEM)
     dma = pltpu.SemaphoreType.DMA
     many = max(16, nb // 16 * ns)
+    spec = pl.BlockSpec((parts, 1, rows, 128), lambda i, j: (0, jnp.minimum(i, docs - 1), 0, j))
+    row = jax.ShapeDtypeStruct(x.shape, BF)
     return pl.pallas_call(
-        functools.partial(final_kernel, nb, ns, rank),
-        in_specs=[any_spec, vmem] + [any_spec] * 8 + [vmem] * 3,
-        out_specs=[any_spec, vmem],
-        out_shape=[jax.ShapeDtypeStruct(x.shape, BF), jax.ShapeDtypeStruct((16, 8, 128), F32)],
-        scratch_shapes=[pltpu.VMEM(x.shape, BF), pltpu.VMEM(x.shape, F32), pltpu.VMEM((3, ns, docs, rows, w), BF),]
+        functools.partial(backward_kernel, nb, ns, rank, size, tile),
+        grid=(docs + 1, w // 128),
+        in_specs=[pl.BlockSpec(memory_space=pltpu.SMEM)] + [spec] * 5
+        + [pl.BlockSpec((1, 1, 2, n), lambda i, j: (jnp.minimum(i, docs - 1), j, 0, 0))]
+        + [any_spec] * 2 + [vmem] + [any_spec] * 5 + [vmem] * 3,
+        out_specs=[any_spec, any_spec, vmem],
+        out_shape=[row, row, jax.ShapeDtypeStruct((16, 8, 128), F32)],
+        scratch_shapes=[pltpu.VMEM((128, n), F32), pltpu.VMEM((docs, 3, parts, rows, w), BF),
+                        pltpu.VMEM(x.shape, BF), pltpu.VMEM(x.shape, F32), pltpu.VMEM((3, ns, docs, rows, w), BF)]
         + [pltpu.VMEM(wq.shape, BF)] * 3
         + [pltpu.VMEM(low.shape, BF), pltpu.VMEM(x.shape, BF)] + [pltpu.VMEM((128, d), F32)] * 3
         + [pltpu.VMEM((16, 8, 128), F32), pltpu.VMEM((16, 8, 128), F32), pltpu.VMEM((nb // 16 * ns, 8, 128), F32),
-           dma((6,)), dma((3, docs, ns)), dma((3, docs, ns)), dma((docs,)), dma((docs,)), dma((3, many)), dma((3, many))],
-        compiler_params=pltpu.CompilerParams(collective_id=3, has_side_effects=True, vmem_limit_bytes=60 << 20),
-        name="projection_gradients",
-    )(x, gain, dq, dk, dv, rg, low, wq, wk, wv, down, upq, upv)
+           pltpu.VMEM((16, 8, 128), F32),
+           dma((6,)), dma((3, docs, ns)), dma((3, docs, ns)), dma((docs, CUTS)), dma((docs, CUTS)), dma((docs,)), dma((docs,)),
+           dma((3, many)), dma((3, many))],
+        compiler_params=pltpu.CompilerParams(collective_id=3, has_side_effects=True, vmem_limit_bytes=62 << 20),
+        name="backward",
+    )(layout, q, k, v, o, g, lse, top, x, gain, rg, low, wq, wk, wv, down, upq, upv)
 
 
 def local(
@@ -842,25 +857,18 @@
     down = jnp.pad(jnp.concatenate([query_down_adapter, value_down_adapter], axis=1), ((0, 0), (0, 128 - 2 * rank)))
     upq = jnp.pad((ADAPTER_SCALE * query_up_adapter).astype(BF), ((0, 128 - rank), (0, 0)))
     upv = jnp.pad((ADAPTER_SCALE * value_up_adapter).astype(BF), ((rank, 128 - 2 * rank), (0, 0)))
-    where = jnp.argsort(layout).astype(jnp.int32)
     gain1 = attention_norm_gain[None]
     gain2 = feedforward_norm_gain[None]
 
     q, k, v, low, x, wq, wk, wv, wo = project(
         nb, ns, tokens, query_weight, key_weight, value_weight, attention_output_weight, gain1, down,
         jnp.stack([upq, jnp.zeros_like(upq), upv]))
-    att, lse, cot, w_up = attention_forward(nb, ns, where, q, k, v, cotangent, up_weight, size)
+    att, lse, cot, w_up = attention_forward(nb, ns, layout, q, k, v, cotangent, up_weight, size)
     out, rg, mix = middle(nb, ns, x, att, cotangent, cot, gain2, wo.reshape(d, d), w_up, down_weight)
-    swap = []
-    for b in range(nb):
-        for s in range(ns):
-            if b % 2 != s % 2:
-                b2, s2 = trade(b, s)
-                swap.append((b * ns + s, b2 * ns + s2))
     stays = lax.axis_index("batch") % 2 == lax.axis_index("seq") % 2
-    layer_out = jnp.where(stays, out, lax.ppermute(out, AXES, swap))
-    dq, dk, dv = attention_backward(where, q, k, v, att, mix, lse, size)
-    input_grad, sums = final(nb, ns, rank, x, gain1, dq, dk, dv, rg, low, wq, wk, wv, down, upq, upv)
+    got, input_grad, sums = backward(
+        nb, ns, rank, layout, q, k, v, att, mix, lse, out, x, gain1, rg, low, wq, wk, wv, down, upq, upv, size)
+    layer_out = jnp.where(stays, out, got)
     sums = sums.reshape(2, d // 128, 2 * rank, 128).transpose(0, 2, 1, 3).reshape(2, 2 * rank, d)
     return (layer_out, input_grad, sums[0, :rank].T, sums[1, :rank], sums[0, rank:].T, sums[1, rank:])
 

time: 332 us -> 316 us (0.952)
  Pallas kernels: 315 us -> 303 us
    pallas_call x2 -> x1, Pallas kernels: 103 us -> 91.3 us  [backward(): pl.pallas_call(functools.partial(backward_kernel, nb, ns, rank, size, til...]
  transfers between devices with their start and end apart: 1 -> 0, of which waited for: 0 -> 0; matrix products, arithmetic and copies ran while one was open for 0% -> 0% of each run, Pallas kernels for 31% -> 0%
where the time goes in v1:
time: 316 us; the launch traced here: 315 us
  Pallas kernels  303 us (96%)
  other arithmetic  7.19 us (2%)
  local copies, waits for them, and re-layouts  4.24 us (1%)
    pallas_call x1, Pallas kernels, backward(): pl.pallas_call(functools.partial(backward_kernel, nb, ns, rank, size, til...  91.3 us
    pallas_call x1, Pallas kernels, middle(): pl.pallas_call(functools.partial(middle_kernel, nb, ns), in_specs=[any_sp...  85.7 us
    pallas_call x1, Pallas kernels, project(): pl.pallas_call(functools.partial(project_kernel, nb, ns), in_specs=[any_s...  67.9 us
    pallas_call x1, Pallas kernels, attention_forward(): pl.pallas_call(functools.partial(attention_forward_kernel, nb, ns, size,...  57.8 us

profile of v1, /device:TPU:1, one launch (start us, length us, event | category | flops | bytes accessed | tf_op | source)
XLA Modules:
  0.0 314.9 jit_solution(2453090465953446402)
XLA Ops:
  0.6 0.7 broadcast_multiply_fusion
  1.3 0.7 broadcast_multiply_fusion.1
  2.0 0.9 fusion
  3.0 0.1 pad.16.clone
  3.0 1.0 pad_maximum_fusion.ups_ref
  4.1 0.7 pad_maximum_fusion.1
  4.8 0.2 copy.23
  5.0 0.8 pad.12.down_ref
  5.7 67.9 %projections.1 = (bf16[2,3,512,512]{3,2,1,0:T(8,128)(2,1)}, bf16[2,3,512,512]{3,2,1,0:T(8,128)(2,1)}, bf16[2,3,512,512]{3,2,1,0:T(8,128)(2,1)}, bf16[3,512,128]{...) custom-call(bf16[3,512,1024]{2,1,0:T(8,128)(2,1)} %x_hbm.1, ...), custom_call_target="tpu_custom_call" | custom-call | tf_op jit(solution)/shard_map/projections/pallas_call | solution.py:296
  73.6 57.8 %attention_forward.1 = (bf16[2,3,512,512]{3,2,1,0:T(8,128)(2,1)}, f32[3,4,2,1024]{3,2,1,0:T(2,128)}, bf16[3,512,1024]{2,1,0:T(8,128)(2,1)}, bf16[16,64,4096]{2,1,0:T(8,128)(2,1)}) custom-call(s32[4]{0:T(128)} %layout.3, bf16[2,3,512,512]{3,2,1,0:T(8,128)(2,1)} %get-tuple-element.26.q_ref, bf16[2,3,512,512]{3,2,1,0:T(8,128)(2,1)} %get-tuple-element.27.k_ref, ...), custom_call_target="tpu_custom_call" | custom-call | tf_op jit(solution)/shard_map/attention_forward/pallas_call | solution.py:420
  131.4 85.7 %feed_forward.1 = (bf16[3,512,1024]{2,1,0:T(8,128)(2,1)}, f32[3,512,1024]{2,1,0:T(8,128)}, bf16[2,3,512,512]{3,2,1,0:T(8,128)(2,1)}) custom-call(bf16[3,512,1024]{2,1,0:T(8,128)(2,1)} %get-tuple-element.25.x_hbm, bf16[2,3,512,512]{3,2,1,0:T(8,128)(2,1)} %get-tuple-element.29.att_hbm.o_ref, bf16[3,512,1024]{2,1,0:T(8,128)(2,1)} %kept_hbm.1, ...), custom_call_target="tpu_custom_call" | custom-call | tf_op jit(solution)/shard_map/feed_forward/pallas_call | solution.py:576
  217.1 91.3 %backward.1 = (bf16[3,512,1024]{2,1,0:T(8,128)(2,1)}, bf16[3,512,1024]{2,1,0:T(8,128)(2,1)}, f32[16,8,128]{2,1,0:T(8,128)}) custom-call(s32[4]{0:T(128)} %layout.3, bf16[2,3,512,512]{3,2,1,0:T(8,128)(2,1)} %get-tuple-element.26.q_ref, bf16[2,3,512,512]{3,2,1,0:T(8,128)(2,1)} %get-tuple-element.27.k_ref, bf16[2,3,512,512]{3,2,1,0:T(8,128)(2,1)} %get-tuple-element.28.v_ref, ...), custom_call_target="tpu_custom_call" | custom-call | tf_op jit(solution)/shard_map/backward/pallas_call | solution.py:827
  308.5 0.0 copy-start.1
  308.5 0.0 copy-start
  308.5 4.0 %broadcast_select_fusion = bf16[3,512,1024]{2,1,0:T(8,128)(2,1)} fusion(bf16[3,512,1024]{2,1,0:T(8,128)(2,1)} %get-tuple-element.33.top_hbm, bf16[3,512,1024]{2,1,0:T(8,128)(2,1)} %get-tuple-element.41, pred[]{:T(512)S(6)} %eq.6), kind=kLoop, calls=%fused_computation | loop fusion | flops 1572864 | bytes 9437185 | tf_op jit(solution)/shard_map/jit(_where)/select_n | solution.py:871
  312.6 0.0 copy-done.1
  312.6 0.6 slice_bitcast_fusion
  313.2 0.0 copy-done
  313.2 1.7 copy.25
Async XLA Ops:
  308.5 4.1 %copy-start.1 = (f32[16,8,128]{2,1,0:T(8,128)S(1)}, f32[16,8,128]{2,1,0:T(8,128)}, u32[]{:S(2)}) copy-start(f32[16,8,128]{2,1,0:T(8,128)} %get-tuple-element.43) | copy-start | bytes 196612
  308.5 4.7 %copy-start = (bf16[3,512,1024]{2,1,0:T(8,128)(2,1)S(1)}, bf16[3,512,1024]{2,1,0:T(8,128)(2,1)}, u32[]{:S(2)}) copy-start(bf16[3,512,1024]{2,1,0:T(8,128)(2,1)} %get-tuple-element.61) | copy-start | bytes 9437188

commit v2 on v1

--- a/solution.py
+++ b/solution.py
@@ -182,131 +182,6 @@
         call()
 
 
-def project_kernel(nb, ns, x_hbm, wq_ref, wk_ref, wv_ref, wo_ref, gain_ref, down_ref, ups_ref,
-                   q_out, k_out, v_out, low_out, x_out, wq_out, wk_out, wv_out, wo_out,
-                   xs, n1s, stage, lows, ws, send, recv, xsend, xrecv, osend, orecv, local_sem):
-    docs, rows, d = x_hbm.shape
-    w = d // ns
-    p = Place(nb, ns)
-    others = [p.peer(r) for r in range(1, ns)]
-    p.greet(p.gather_ways() + [(p.partner, jnp.logical_not(p.stays))] + [(o, None) for o in others])
-
-    def x_remote(i):
-        return pltpu.make_async_remote_copy(
-            src_ref=x_hbm.at[i], dst_ref=xs.at[i], send_sem=xsend.at[i], recv_sem=xrecv.at[i],
-            device_id=p.partner, device_id_type=MESH)
-
-    def x_local(i):
-        return pltpu.make_async_copy(x_hbm.at[i], xs.at[i], xrecv.at[i])
-
-    def x_keep(i):
-        return pltpu.make_async_copy(xs.at[i], x_out.at[i], local_sem.at[i])
-
-    for i in range(docs):
-        pl.when(p.stays)(lambda i=i: x_local(i).start())
-        pl.when(jnp.logical_not(p.stays))(lambda i=i: x_remote(i).start())
-
-    def first(i):
-        pl.when(p.stays)(lambda: x_local(i).wait())
-        pl.when(jnp.logical_not(p.stays))(lambda: x_remote(i).wait())
-        x_keep(i).start()
-        xh, _ = normalise(xs[i].astype(F32))
-        n1 = (xh * gain_ref[...]).astype(BF)
-        n1s[i] = n1
-        lows[i] = dot(n1, down_ref[...]).astype(BF)
-
-    outs = (q_out, k_out, v_out)
-
-    def away(part, i, r):
-        return pltpu.make_async_remote_copy(
-            src_ref=stage.at[part, i, flip(p.part, r)], dst_ref=outs[part].at[p.part, i],
-            send_sem=osend.at[part, i, r], recv_sem=orecv.at[part, i, r],
-            device_id=p.peer(r), device_id_type=MESH)
-
-    def home(part, i):
-        return pltpu.make_async_copy(stage.at[part, i, p.part], outs[part].at[p.part, i], osend.at[part, i, 0])
-
-    def product(part, i):
-        y = dot(n1s[i], ws[part].reshape(d, d)) + dot(lows[i], ups_ref[part])
-        y = y.astype(BF)
-        for g in range(ns):
-            stage[part, i, g] = y[:, g * w:(g + 1) * w]
-        for n in range(3):
-            @pl.when(part == n)
-            def _():
-                home(n, i).start()
-                for r in range(1, ns):
-                    away(n, i, r).start()
-
-    gathers = [Gather(p, own, full, send.at[n], recv.at[n]) for n, (own, full) in enumerate(
-        ((wq_ref, ws.at[0]), (wk_ref, ws.at[1]), (wv_ref, ws.at[2]), (wo_ref, ws.at[3])))]
-    keeps = [pltpu.make_async_copy(ws.at[n], out, local_sem.at[docs + n])
-             for n, out in enumerate((wq_out, wk_out, wv_out, wo_out))]
-    low_keep = pltpu.make_async_copy(lows, low_out, local_sem.at[docs + 4])
-
-    lists = [g.steps() for g in gathers]
-    delays = (0, 0, 2, 4)
-    ready = [len(lists[0]) - 1 + delay for delay in delays]
-
-    def slot(t):
-        for n, steps in enumerate(lists):
-            if 0 <= t - delays[n] < len(steps):
-                steps[t - delays[n]]()
-            if t == ready[n]:
-                keeps[n].start()
-
-    for t in range(ready[0] + 1):
-        slot(t)
-    places = {2 * docs - 5 + 2 * n: t for n, t in enumerate(range(ready[0] + 1, ready[3] + 1))}
-
-    def one_product(n, carry):
-        early = n < 2 * docs
-        part = jnp.where(early, n % 2, 2)
-        i = jnp.where(early, n // 2, n - 2 * docs)
-        pl.when(early & (part == 0))(lambda: first(i))
-        product(part, i)
-        for at, t in places.items():
-            pl.when(n == at)(functools.partial(slot, t))
-        return carry
-
-    lax.fori_loop(0, 3 * docs, one_product, 0)
-    low_keep.start()
-    for part in range(3):
-        for i in range(docs):
-            home(part, i).wait()
-            for r in range(1, ns):
-                away(part, i, r).wait()
-    for i in range(docs):
-        x_keep(i).wait()
-    for keep in keeps:
-        keep.wait()
-    low_keep.wait()
-    for g in gathers:
-        g.drain()
-
-
-def project(nb, ns, x, wq, wk, wv, wo, gain, down, ups):
-    docs, rows, d = x.shape
-    w = d // ns
-    any_spec = pl.BlockSpec(memory_space=pl.ANY)
-    vmem = pl.BlockSpec(memory_space=pltpu.VMEM)
-    head = jax.ShapeDtypeStruct((ns, docs, rows, w), BF)
-    full = jax.ShapeDtypeStruct((nb,) + wq.shape, BF)
-    dma = pltpu.SemaphoreType.DMA
-    return pl.pallas_call(
-        functools.partial(project_kernel, nb, ns),
-        in_specs=[any_spec] * 5 + [vmem] * 3,
-        out_specs=[any_spec] * 9,
-        out_shape=[head] * 3 + [jax.ShapeDtypeStruct((docs, rows, 128), BF), jax.ShapeDtypeStruct(x.shape, BF)] + [full] * 4,
-        scratch_shapes=[pltpu.VMEM(x.shape, BF), pltpu.VMEM(x.shape, BF), pltpu.VMEM((3, docs, ns, rows, w), BF),
-                        pltpu.VMEM((docs, rows, 128), BF)] + [pltpu.VMEM((4,) + full.shape, BF)] + [
-                        dma((4, 4, nb)), dma((4, nb)), dma((docs,)), dma((docs,)),
-                        dma((3, docs, ns)), dma((3, docs, ns)), dma((docs + 5,))],
-        compiler_params=pltpu.CompilerParams(collective_id=0, has_side_effects=True, vmem_limit_bytes=60 << 20),
-        name="projections",
-    )(x, wq, wk, wv, wo, gain, down, ups)
-
-
 def chosen(blocks, tests):
     out = blocks[0]
     for block, test in zip(blocks[1:], tests[1:]):
@@ -326,53 +201,19 @@
         store(t, chosen(pieces, [layout[t] == p for p in range(blocks)]))
 
 
-PACE = 4
-
-
-def attention_forward_kernel(nb, ns, size, tile, layout, q_ref, k_ref, v_ref, cot_hbm, up_hbm,
-                             o_ref, lse_ref, cot_out, up_out, own, send, recv, csend, crecv, own_sem):
-    docs = cot_hbm.shape[0]
-    p = Place(nb, ns)
-    step = pl.program_id(0) * pl.num_programs(1) + pl.program_id(1)
-    steps = docs * (up_hbm.shape[0] * nb // ns // 128)
-    gather = Gather(p, own, up_out, send, recv)
-    events = gather.steps()
-
-    def cross(i):
-        return pltpu.make_async_remote_copy(
-            src_ref=cot_hbm.at[i], dst_ref=cot_out.at[i], send_sem=csend.at[i], recv_sem=crecv.at[i],
-            device_id=p.partner, device_id_type=MESH)
-
-    def begin():
-        fetch = pltpu.make_async_copy(up_hbm, own, own_sem)
-        fetch.start()
-        p.greet(p.gather_ways() + [(p.partner, jnp.logical_not(p.stays))])
-        fetch.wait()
-        events[0]()
-        for i in range(docs):
-            pl.when(jnp.logical_not(p.stays))(lambda i=i: cross(i).start())
-
-    def end():
-        for n, event in enumerate(events):
-            if n and PACE * n >= steps:
-                event()
-        for i in range(docs):
-            pl.when(jnp.logical_not(p.stays))(lambda i=i: cross(i).wait())
-        gather.drain()
-
-    pl.when(step == 0)(begin)
-    for n, event in enumerate(events):
-        if n and PACE * n < steps:
-            pl.when(step == PACE * n)(event)
-
+def attend(layout, qkv, out, lse_ref, doc, pair, size, tile):
+    parts, rows = qkv.shape[1], qkv.shape[3]
+    n = parts * rows
+    blocks, per = n // size, rows // size
+    lanes = pl.ds(pl.multiple_of(pair * 128, 128), 128)
+
+    def in_order(t):
+        stored = [qkv[t, b // per, doc, b % per * size:(b % per + 1) * size, lanes] for b in range(blocks)]
+        return jnp.concatenate([chosen(stored, [layout[b] == p for b in range(blocks)]) for p in range(blocks)], axis=0)
+
+    q, k, v = in_order(0), in_order(1), in_order(2)
+    vt = v.T
     lane = lax.broadcasted_iota(jnp.int32, (1, 128), 1)
-    parts, rows = q_ref.shape[0], q_ref.shape[2]
-    n = parts * rows
-    blocks = n // size
-    q = picked(q_ref, layout, blocks, size)
-    k = picked(k_ref, layout, blocks, size)
-    v = picked(v_ref, layout, blocks, size)
-    vt = v.T
     c = SCORE_SCALE * LOG2E
     tri = lax.broadcasted_iota(jnp.int32, (tile, tile), 0) <= lax.broadcasted_iota(jnp.int32, (tile, tile), 1)
     work = [(i, h) for i in range(n // tile) for h in range(2)]
@@ -398,50 +239,215 @@
         mixed[i, h] = o * (1.0 / l)
         lses[h].append(m + jnp.log2(l))
     outs = [jnp.concatenate([mixed[i, 0], mixed[i, 1]], axis=0).T.astype(BF) for i in range(n // tile)]
-    per = rows // size
-
-    def store(t, piece):
-        o_ref[t // per, 0, t % per * size:(t % per + 1) * size, :] = piece
+
+    def store(b, piece):
+        out[b // per, doc, b % per * size:(b % per + 1) * size, lanes] = piece
 
     put_back(jnp.concatenate(outs, axis=0), layout, blocks, size, store)
     for h in range(2):
-        lse_ref[0, 0, h:h + 1, :] = jnp.concatenate(lses[h], axis=1)
-
-    pl.when(step == steps - 1)(end)
-
-
-def attention_forward(nb, ns, layout, q, k, v, cot, up, size, tile=256):
-    parts, docs, rows, w = q.shape
+        lse_ref[doc, pair, h:h + 1, :] = jnp.concatenate(lses[h], axis=1)
+
+
+PACE = 4
+
+
+def front_kernel(nb, ns, size, tile, layout, x_hbm, cot_hbm, wq_ref, wk_ref, wv_ref, wo_ref, up_hbm, gain_ref, down_ref, ups_ref,
+                 qkv_out, att_out, mixed_out, lse_ref, low_out, x_out, cot_out, wq_out, wk_out, wv_out, wo_out, up_out,
+                 xs, n1s, stage, qkv, att, lows, ws, own, send, recv, usend, urecv, xsend, xrecv, csend, crecv,
+                 osend, orecv, asend, arecv, local_sem, qkv_sem, att_sem):
+    docs, rows, d = x_hbm.shape
+    w = d // ns
     pairs = w // 128
-    n = parts * rows
-    spec = pl.BlockSpec((parts, 1, rows, 128), lambda d, p: (0, d, 0, p))
+    p = Place(nb, ns)
+    fetch = pltpu.make_async_copy(up_hbm, own, local_sem.at[docs + 5])
+    fetch.start()
+    p.greet(p.gather_ways() + [(p.partner, jnp.logical_not(p.stays))] + [(p.peer(r), None) for r in range(1, ns)])
+
+    def x_remote(i):
+        return pltpu.make_async_remote_copy(
+            src_ref=x_hbm.at[i], dst_ref=xs.at[i], send_sem=xsend.at[i], recv_sem=xrecv.at[i],
+            device_id=p.partner, device_id_type=MESH)
+
+    def cot_remote(i):
+        return pltpu.make_async_remote_copy(
+            src_ref=cot_hbm.at[i], dst_ref=cot_out.at[i], send_sem=csend.at[i], recv_sem=crecv.at[i],
+            device_id=p.partner, device_id_type=MESH)
+
+    def x_local(i):
+        return pltpu.make_async_copy(x_hbm.at[i], xs.at[i], xrecv.at[i])
+
+    def x_keep(i):
+        return pltpu.make_async_copy(xs.at[i], x_out.at[i], local_sem.at[i])
+
+    for i in range(docs):
+        pl.when(p.stays)(lambda i=i: x_local(i).start())
+        pl.when(jnp.logical_not(p.stays))(lambda i=i: x_remote(i).start())
+    for i in range(docs):
+        pl.when(jnp.logical_not(p.stays))(lambda i=i: cot_remote(i).start())
+
+    def first(i):
+        pl.when(p.stays)(lambda: x_local(i).wait())
+        pl.when(jnp.logical_not(p.stays))(lambda: x_remote(i).wait())
+        x_keep(i).start()
+        xh, _ = normalise(xs[i].astype(F32))
+        n1 = (xh * gain_ref[...]).astype(BF)
+        n1s[i] = n1
+        lows[i] = dot(n1, down_ref[...]).astype(BF)
+
+    def away(part, i, r):
+        return pltpu.make_async_remote_copy(
+            src_ref=stage.at[part, i, flip(p.part, r)], dst_ref=qkv.at[part, p.part, i],
+            send_sem=osend.at[part, i, r], recv_sem=orecv.at[part, i, r],
+            device_id=p.peer(r), device_id_type=MESH)
+
+    def product(part, i):
+        y = dot(n1s[i], ws[part].reshape(d, d)) + dot(lows[i], ups_ref[part])
+        y = y.astype(BF)
+        for g in range(ns):
+            piece = y[:, g * w:(g + 1) * w]
+
+            @pl.when(p.part == g)
+            def _():
+                qkv[part, p.part, i] = piece
+
+            @pl.when(p.part != g)
+            def _():
+                stage[part, i, g] = piece
+        for r in range(1, ns):
+            away(part, i, r).start()
+
+    gathers = [Gather(p, own_ref, ws.at[n], send.at[n], recv.at[n])
+               for n, own_ref in enumerate((wq_ref, wk_ref, wv_ref, wo_ref))]
+    keeps = [pltpu.make_async_copy(ws.at[n], out, local_sem.at[docs + n])
+             for n, out in enumerate((wq_out, wk_out, wv_out, wo_out))]
+    low_keep = pltpu.make_async_copy(lows, low_out, local_sem.at[docs + 4])
+    up_steps = Gather(p, own, up_out, usend, urecv).steps()
+
+    lists = [g.steps() for g in gathers]
+    delays = (0, 0, 2, 4)
+    ready = [len(lists[0]) - 1 + delay for delay in delays]
+
+    def slot(t):
+        for n, steps in enumerate(lists):
+            if 0 <= t - delays[n] < len(steps):
+                steps[t - delays[n]]()
+            if t == ready[n]:
+                keeps[n].start()
+        if t == ready[0] + 1:
+            fetch.wait()
+            up_steps[0]()
+
+    for t in range(ready[0] + 1):
+        slot(t)
+    places = {2 * docs - 5 + 2 * n: t for n, t in enumerate(range(ready[0] + 1, ready[3] + 1))}
+
+    def one_product(n, carry):
+        early = n < 2 * docs
+        part = jnp.where(early, n % 2, 2)
+        i = jnp.where(early, n // 2, n - 2 * docs)
+        pl.when(early & (part == 0))(lambda: first(i))
+        product(part, i)
+        for at, t in places.items():
+            pl.when(n == at)(functools.partial(slot, t))
+        return carry
+
+    lax.fori_loop(0, 3 * docs, one_product, 0)
+    low_keep.start()
+
+    def qkv_keep(i):
+        return pltpu.make_async_copy(qkv.at[:, :, i], qkv_out.at[:, :, i], qkv_sem.at[i])
+
+    def att_keep(i):
+        return pltpu.make_async_copy(att.at[:, i], att_out.at[:, i], att_sem.at[i, 0])
+
+    def att_home(i):
+        return pltpu.make_async_copy(att.at[p.part, i], mixed_out.at[p.part, i], att_sem.at[i, 1])
+
+    def att_away(i, r):
+        return pltpu.make_async_remote_copy(
+            src_ref=att.at[flip(p.part, r), i], dst_ref=mixed_out.at[p.part, i], send_sem=asend.at[i, r],
+            recv_sem=arecv.at[i, r], device_id=p.peer(r), device_id_type=MESH)
+
+    def one_pair(m, carry):
+        doc, pair = m // pairs, m % pairs
+        for n in range(1, len(up_steps)):
+            if PACE * (n - 1) < docs * pairs:
+                pl.when(m == PACE * (n - 1))(up_steps[n])
+
+        @pl.when(pair == 0)
+        def _():
+            for part in range(3):
+                for r in range(1, ns):
+                    away(part, doc, r).wait()
+            qkv_keep(doc).start()
+
+        attend(layout, qkv, att, lse_ref, doc, pair, size, tile)
+
+        @pl.when(pair == pairs - 1)
+        def _():
+            att_keep(doc).start()
+            att_home(doc).start()
+            for r in range(1, ns):
+                att_away(doc, r).start()
+
+        return carry
+
+    lax.fori_loop(0, docs * pairs, one_pair, 0)
+    for n in range(1, len(up_steps)):
+        if PACE * (n - 1) >= docs * pairs:
+            up_steps[n]()
+    for i in range(docs):
+        x_keep(i).wait()
+        pl.when(jnp.logical_not(p.stays))(lambda i=i: cot_remote(i).wait())
+        qkv_keep(i).wait()
+        att_keep(i).wait()
+        att_home(i).wait()
+        for r in range(1, ns):
+            att_away(i, r).wait()
+    for keep in keeps:
+        keep.wait()
+    low_keep.wait()
+    for g in gathers + [Gather(p, own, up_out, usend, urecv)]:
+        g.drain()
+
+
+def front(nb, ns, layout, x, cot, wq, wk, wv, wo, up, gain, down, ups, size, tile=256):
+    docs, rows, d = x.shape
+    w = d // ns
+    n = rows * ns
     any_spec = pl.BlockSpec(memory_space=pl.ANY)
+    vmem = pl.BlockSpec(memory_space=pltpu.VMEM)
     dma = pltpu.SemaphoreType.DMA
+    like = lambda *shape: jax.ShapeDtypeStruct(shape, BF)
+    heads = (ns, docs, rows, w)
+    outs = [like(3, *heads), like(*heads), like(*heads), jax.ShapeDtypeStruct((docs, w // 128, 2, n), F32),
+            like(docs, rows, 128), like(*x.shape), like(*x.shape)] + [like(nb, *wq.shape)] * 4 + [like(nb, *up.shape)]
     return pl.pallas_call(
-        functools.partial(attention_forward_kernel, nb, ns, size, tile),
-        grid=(docs, pairs),
-        in_specs=[pl.BlockSpec(memory_space=pltpu.SMEM), spec, spec, spec] + [any_spec] * 2,
-        out_specs=[spec, pl.BlockSpec((1, 1, 2, n), lambda d, p: (d, p, 0, 0))] + [any_spec] * 2,
-        out_shape=[jax.ShapeDtypeStruct((parts, docs, rows, w), BF),
-                   jax.ShapeDtypeStruct((docs, pairs, 2, n), F32),
-                   jax.ShapeDtypeStruct(cot.shape, BF),
-                   jax.ShapeDtypeStruct((nb,) + up.shape, BF)],
-        scratch_shapes=[pltpu.VMEM(up.shape, BF), dma((4, nb)), dma((nb,)), dma((docs,)), dma((docs,)), dma],
-        compiler_params=pltpu.CompilerParams(collective_id=1, has_side_effects=True, vmem_limit_bytes=60 << 20),
-        name="attention_forward",
-    )(layout, q, k, v, cot, up)
+        functools.partial(front_kernel, nb, ns, size, tile),
+        in_specs=[pl.BlockSpec(memory_space=pltpu.SMEM)] + [any_spec] * 7 + [vmem] * 3,
+        out_specs=[any_spec] * 3 + [vmem] + [any_spec] * 8,
+        out_shape=outs,
+        scratch_shapes=[pltpu.VMEM(x.shape, BF), pltpu.VMEM(x.shape, BF), pltpu.VMEM((3, docs, ns, rows, w), BF),
+                        pltpu.VMEM((3,) + heads, BF), pltpu.VMEM(heads, BF), pltpu.VMEM((docs, rows, 128), BF),
+                        pltpu.VMEM((4, nb) + wq.shape, BF), pltpu.VMEM(up.shape, BF),
+                        dma((4, 4, nb)), dma((4, nb)), dma((4, nb)), dma((nb,)), dma((docs,)), dma((docs,)),
+                        dma((docs,)), dma((docs,)), dma((3, docs, ns)), dma((3, docs, ns)), dma((docs, ns)), dma((docs, ns)),
+                        dma((docs + 6,)), dma((docs,)), dma((docs, 2))],
+        compiler_params=pltpu.CompilerParams(collective_id=0, has_side_effects=True, vmem_limit_bytes=62 << 20),
+        name="front",
+    )(layout, x, cot, wq, wk, wv, wo, up, gain, down, ups)
 
 
 def middle_kernel(nb, ns, x_hbm, att_hbm, kept_hbm, cot_hbm, gain_ref, wo_hbm, up_hbm, down_hbm,
                   out_hbm, rg_hbm, mix_hbm,
                   xs, atts, cots, wos, downs, ups, acc, xhs, dn, n2s, invs, us, gs,
-                  send, recv, asend, arecv, msend, mrecv, load, store):
+                  send, recv, msend, mrecv, load, store):
     docs, rows, d = x_hbm.shape
     w = d // ns
     p = Place(nb, ns)
     held = down_hbm.shape[0]
     chunk = 2 * held
-    loads = [pltpu.make_async_copy(wo_hbm, wos, load.at[0])]
+    loads = [pltpu.make_async_copy(wo_hbm, wos, load.at[0]), pltpu.make_async_copy(att_hbm, atts, load.at[3 + docs])]
     for i in range(docs):
         loads.append(pltpu.make_async_copy(x_hbm.at[i], xs.at[i], load.at[1 + i]))
     loads.append(pltpu.make_async_copy(up_hbm, ups, load.at[1 + docs]))
@@ -457,26 +463,9 @@
 
     gather = Gather(p, down_hbm, downs, send, recv)
 
-    def att_away(i, r):
-        return pltpu.make_async_remote_copy(
-            src_ref=att_hbm.at[flip(p.part, r), i], dst_ref=atts.at[p.part, i], send_sem=asend.at[i, r],
-            recv_sem=arecv.at[i, r], device_id=p.peer(r), device_id_type=MESH)
-
-    def att_home(i):
-        return pltpu.make_async_copy(att_hbm.at[p.part, i], atts.at[p.part, i], arecv.at[i, 0])
-
-    for i in range(docs):
-        att_home(i).start()
-        for r in range(1, ns):
-            att_away(i, r).start()
     gather.start()
     for copy in loads[:-1]:
         copy.wait()
-    for i in range(docs):
-        att_home(i).wait()
-        for r in range(1, ns):
-            att_away(i, r).wait()
-
     def rows_of(i):
         return pl.ds(pl.multiple_of(i * rows, rows), rows)
 
@@ -585,8 +574,7 @@
                         pltpu.VMEM((n, d), F32), pltpu.VMEM((n, d), F32), pltpu.VMEM((n, d), BF),
                         pltpu.VMEM((n, 128), F32), pltpu.VMEM((2, rows, 2 * down.shape[0]), F32),
                         pltpu.VMEM((2, rows, 2 * down.shape[0]), F32),
-                        dma((4, nb)), dma((nb,)), dma((docs, ns)), dma((docs, ns)),
-                        dma((docs, ns)), dma((docs, ns)), dma((3 + docs,)), dma((3, docs))],
+                        dma((4, nb)), dma((nb,)), dma((docs, ns)), dma((docs, ns)), dma((4 + docs,)), dma((3, docs))],
         compiler_params=pltpu.CompilerParams(collective_id=2, has_side_effects=True, vmem_limit_bytes=63 << 20),
         name="feed_forward",
     )(x, att, kept, cot, gain, wo, up, down)
@@ -756,12 +744,12 @@
 
 
 def attention_gradients(layout, q_ref, k_ref, v_ref, o_ref, g_ref, lse_ref, stage, dqt, doc, pair, size, tile):
-    parts, rows = q_ref.shape[0], q_ref.shape[2]
+    parts, rows = o_ref.shape[0], o_ref.shape[2]
     n = parts * rows
     blocks, per = n // size, rows // size
-    q = picked(q_ref, layout, blocks, size)
-    k = picked(k_ref, layout, blocks, size)
-    v = picked(v_ref, layout, blocks, size)
+    q = picked(q_ref.at[0], layout, blocks, size)
+    k = picked(k_ref.at[0], layout, blocks, size)
+    v = picked(v_ref.at[0], layout, blocks, size)
     o = picked(o_ref, layout, blocks, size)
     g = picked(g_ref, layout, blocks, size)
     kt = k.T
@@ -813,9 +801,9 @@
         put_back(value, layout, blocks, size, store)
 
 
-def backward(nb, ns, rank, layout, q, k, v, o, g, lse, top, x, gain, rg, low, wq, wk, wv, down, upq, upv, size, tile=256):
+def backward(nb, ns, rank, layout, qkv, o, g, lse, top, x, gain, rg, low, wq, wk, wv, down, upq, upv, size, tile=256):
     docs, rows, d = x.shape
-    parts = q.shape[0]
+    parts = o.shape[0]
     w = d // ns
     n = parts * rows
     any_spec = pl.BlockSpec(memory_space=pl.ANY)
@@ -824,10 +812,14 @@
     many = max(16, nb // 16 * ns)
     spec = pl.BlockSpec((parts, 1, rows, 128), lambda i, j: (0, jnp.minimum(i, docs - 1), 0, j))
     row = jax.ShapeDtypeStruct(x.shape, BF)
+
+    def third(t):
+        return pl.BlockSpec((1, parts, 1, rows, 128), lambda i, j: (t, 0, jnp.minimum(i, docs - 1), 0, j))
+
     return pl.pallas_call(
         functools.partial(backward_kernel, nb, ns, rank, size, tile),
         grid=(docs + 1, w // 128),
-        in_specs=[pl.BlockSpec(memory_space=pltpu.SMEM)] + [spec] * 5
+        in_specs=[pl.BlockSpec(memory_space=pltpu.SMEM), third(0), third(1), third(2), spec, spec]
         + [pl.BlockSpec((1, 1, 2, n), lambda i, j: (jnp.minimum(i, docs - 1), j, 0, 0))]
         + [any_spec] * 2 + [vmem] + [any_spec] * 5 + [vmem] * 3,
         out_specs=[any_spec, any_spec, vmem],
@@ -842,7 +834,7 @@
            dma((3, many)), dma((3, many))],
         compiler_params=pltpu.CompilerParams(collective_id=3, has_side_effects=True, vmem_limit_bytes=62 << 20),
         name="backward",
-    )(layout, q, k, v, o, g, lse, top, x, gain, rg, low, wq, wk, wv, down, upq, upv)
+    )(layout, qkv, qkv, qkv, o, g, lse, top, x, gain, rg, low, wq, wk, wv, down, upq, upv)
 
 
 def local(
@@ -860,14 +852,13 @@
     gain1 = attention_norm_gain[None]
     gain2 = feedforward_norm_gain[None]
 
-    q, k, v, low, x, wq, wk, wv, wo = project(
-        nb, ns, tokens, query_weight, key_weight, value_weight, attention_output_weight, gain1, down,
-        jnp.stack([upq, jnp.zeros_like(upq), upv]))
-    att, lse, cot, w_up = attention_forward(nb, ns, layout, q, k, v, cotangent, up_weight, size)
-    out, rg, mix = middle(nb, ns, x, att, cotangent, cot, gain2, wo.reshape(d, d), w_up, down_weight)
+    qkv, att, mixed, lse, low, x, cot, wq, wk, wv, wo, w_up = front(
+        nb, ns, layout, tokens, cotangent, query_weight, key_weight, value_weight, attention_output_weight, up_weight,
+        gain1, down, jnp.stack([upq, jnp.zeros_like(upq), upv]), size)
+    out, rg, mix = middle(nb, ns, x, mixed, cotangent, cot, gain2, wo.reshape(d, d), w_up, down_weight)
     stays = lax.axis_index("batch") % 2 == lax.axis_index("seq") % 2
     got, input_grad, sums = backward(
-        nb, ns, rank, layout, q, k, v, att, mix, lse, out, x, gain1, rg, low, wq, wk, wv, down, upq, upv, size)
+        nb, ns, rank, layout, qkv, att, mix, lse, out, x, gain1, rg, low, wq, wk, wv, down, upq, upv, size)
     layer_out = jnp.where(stays, out, got)
     sums = sums.reshape(2, d // 128, 2 * rank, 128).transpose(0, 2, 1, 3).reshape(2, 2 * rank, d)
     return (layer_out, input_grad, sums[0, :rank].T, sums[1, :rank], sums[0, rank:].T, sums[1, rank:])

time: 316 us -> 304 us (0.962)
  Pallas kernels: 303 us -> 291 us
    pallas_call x2 -> x1, Pallas kernels: 126 us -> 111 us  [front(): pl.pallas_call(functools.partial(front_kernel, nb, ns, size, tile), in_sp...]
where the time goes in v2:
time: 304 us; the launch traced here: 303 us
  Pallas kernels  291 us (96%)
  other arithmetic  7.19 us (2%)
  local copies, waits for them, and re-layouts  4.25 us (1%)
    pallas_call x1, Pallas kernels, front(): pl.pallas_call(functools.partial(front_kernel, nb, ns, size, tile), in_sp...  111 us
    pallas_call x1, Pallas kernels, backward(): pl.pallas_call(functools.partial(backward_kernel, nb, ns, rank, size, til...  91.8 us
    pallas_call x1, Pallas kernels, middle(): pl.pallas_call(functools.partial(middle_kernel, nb, ns), in_specs=[any_sp...  88 us

profile of v2, /device:TPU:1, one launch (start us, length us, event | category | flops | bytes accessed | tf_op | source)
XLA Modules:
  0.0 303.3 jit_solution(349600043770447933)
XLA Ops:
  0.6 0.7 broadcast_multiply_fusion
  1.3 0.7 broadcast_multiply_fusion.1
  2.0 0.9 fusion
  3.0 0.1 pad.16.clone
  3.1 1.0 pad_maximum_fusion.ups_ref
  4.1 0.7 pad_maximum_fusion.1
  4.8 0.2 copy.23
  5.0 0.8 pad.12.down_ref
  5.7 111.3 %front.1 = (bf16[3,2,3,512,512]{4,3,2,1,0:T(8,128)(2,1)}, bf16[2,3,512,512]{3,2,1,0:T(8,128)(2,1)}, bf16[2,3,512,512]{3,2,1,0:T(8,128)(2,1)}, f32[3,4,2,1024]{3,...) custom-call(s32[4]{0:T(128)} %layout.3, ...), custom_call_target="tpu_custom_call" | custom-call | tf_op jit(solution)/shard_map/front/pallas_call | solution.py:425
  117.1 88.0 %feed_forward.1 = (bf16[3,512,1024]{2,1,0:T(8,128)(2,1)}, f32[3,512,1024]{2,1,0:T(8,128)}, bf16[2,3,512,512]{3,2,1,0:T(8,128)(2,1)}) custom-call(bf16[3,512,1024]{2,1,0:T(8,128)(2,1)} %get-tuple-element.24.x_hbm, bf16[2,3,512,512]{3,2,1,0:T(8,128)(2,1)} %get-tuple-element.25.att_hbm, bf16[3,512,1024]{2,1,0:T(8,128)(2,1)} %kept_hbm.1, ...), custom_call_target="tpu_custom_call" | custom-call | tf_op jit(solution)/shard_map/feed_forward/pallas_call | solution.py:565
  205.1 91.8 %backward.1 = (bf16[3,512,1024]{2,1,0:T(8,128)(2,1)}, bf16[3,512,1024]{2,1,0:T(8,128)(2,1)}, f32[16,8,128]{2,1,0:T(8,128)}) custom-call(s32[4]{0:T(128)} %layout.3, bf16[3,2,3,512,512]{4,3,2,1,0:T(8,128)(2,1)} %get-tuple-element.30.q_ref.k_ref.v_ref, bf16[3,2,3,512,512]{4,3,2,1,0:T(8,128)(2,1)} %get-tuple-element.30.q_ref.k_ref.v_ref, ...), custom_call_target="tpu_custom_call" | custom-call | tf_op jit(solution)/shard_map/backward/pallas_call | solution.py:819
  297.0 0.0 copy-start.1
  297.0 0.0 copy-start
  297.0 4.0 %broadcast_select_fusion = bf16[3,512,1024]{2,1,0:T(8,128)(2,1)} fusion(bf16[3,512,1024]{2,1,0:T(8,128)(2,1)} %get-tuple-element.29.top_hbm, bf16[3,512,1024]{2,1,0:T(8,128)(2,1)} %get-tuple-element.39, pred[]{:T(512)S(6)} %eq.6), kind=kLoop, calls=%fused_computation | loop fusion | flops 1572864 | bytes 9437185 | tf_op jit(solution)/shard_map/jit(_where)/select_n | solution.py:862
  301.0 0.0 copy-done.1
  301.0 0.6 slice_bitcast_fusion
  301.7 0.0 copy-done
  301.7 1.7 copy.25
Async XLA Ops:
  297.0 4.1 %copy-start.1 = (f32[16,8,128]{2,1,0:T(8,128)S(1)}, f32[16,8,128]{2,1,0:T(8,128)}, u32[]{:S(2)}) copy-start(f32[16,8,128]{2,1,0:T(8,128)} %get-tuple-element.41) | copy-start | bytes 196612
  297.0 4.7 %copy-start = (bf16[3,512,1024]{2,1,0:T(8,128)(2,1)S(1)}, bf16[3,512,1024]{2,1,0:T(8,128)(2,1)}, u32[]{:S(2)}) copy-start(bf16[3,512,1024]{2,1,0:T(8,128)(2,1)} %get-tuple-element.59) | copy-start | bytes 9437188

commit v3 on v2

--- a/solution.py
+++ b/solution.py
@@ -73,16 +73,22 @@
     def peer(self, r):
         return trade(self.doc, flip(self.part, r))
 
-    def greet(self, ways):
+    def hello(self, ways):
         bar = pltpu.get_barrier_semaphore()
         for device, cond in ways:
-            def hello(device=device):
+            def signal(device=device):
                 pl.semaphore_signal(bar, inc=1, device_id=device, device_id_type=MESH)
-            hello() if cond is None else pl.when(cond)(hello)
+            signal() if cond is None else pl.when(cond)(signal)
+
+    def met(self, ways):
         count = 0
         for _, cond in ways:
             count = count + (1 if cond is None else jnp.where(cond, 1, 0))
-        pl.semaphore_wait(bar, count)
+        pl.semaphore_wait(pltpu.get_barrier_semaphore(), count)
+
+    def greet(self, ways):
+        self.hello(ways)
+        self.met(ways)
 
     def gather_ways(self):
         b, s = self.b, self.s
@@ -213,31 +219,39 @@
 
     q, k, v = in_order(0), in_order(1), in_order(2)
     vt = v.T
+    ones = jnp.ones((16, n), BF)
+    vts = [jnp.concatenate([vt[64 * h:64 * h + 64], ones], axis=0) for h in range(2)]
     lane = lax.broadcasted_iota(jnp.int32, (1, 128), 1)
     c = SCORE_SCALE * LOG2E
     tri = lax.broadcasted_iota(jnp.int32, (tile, tile), 0) <= lax.broadcasted_iota(jnp.int32, (tile, tile), 1)
     work = [(i, h) for i in range(n // tile) for h in range(2)]
     lses = [[], []]
     mixed = {}
+    waiting = []
 
     def scores(i, h):
         qm = jnp.where((lane < 64) == (h == 0), q[i * tile:(i + 1) * tile], jnp.zeros((), BF))
         return dot(k[:(i + 1) * tile], qm, NT)
 
-    ahead = scores(*work[0])
+    def settle():
+        i, h, e, m = waiting.pop(0)
+        o = dot(vts[h][:, :(i + 1) * tile], e)
+        l = o[64:65]
+        mixed[i, h] = o[:64] * (1.0 / l)
+        lses[h].append(m + jnp.log2(l))
+
+    ahead = [scores(*work[0]), scores(*work[1])]
     for t, (i, h) in enumerate(work):
-        st = ahead
-        if t + 1 < len(work):
-            ahead = scores(*work[t + 1])
-        kk = (i + 1) * tile
+        st = ahead.pop(0)
+        if t + 2 < len(work):
+            ahead.append(scores(*work[t + 2]))
         diag = jnp.where(tri, st[i * tile:], NEG_FILL)
         st = diag if i == 0 else jnp.concatenate([st[: i * tile], diag], axis=0)
         m = jnp.max(st, axis=0, keepdims=True) * c
-        e = jnp.exp2(st * c - m)
-        l = jnp.sum(e, axis=0, keepdims=True)
-        o = dot(vt[64 * h:64 * h + 64, :kk], e.astype(BF))
-        mixed[i, h] = o * (1.0 / l)
-        lses[h].append(m + jnp.log2(l))
+        waiting.append((i, h, jnp.exp2(st * c - m).astype(BF), m))
+        if t:
+            settle()
+    settle()
     outs = [jnp.concatenate([mixed[i, 0], mixed[i, 1]], axis=0).T.astype(BF) for i in range(n // tile)]
 
     def store(b, piece):
@@ -248,12 +262,27 @@
         lse_ref[doc, pair, h:h + 1, :] = jnp.concatenate(lses[h], axis=1)
 
 
-PACE = 4
-
-
-def front_kernel(nb, ns, size, tile, layout, x_hbm, cot_hbm, wq_ref, wk_ref, wv_ref, wo_ref, up_hbm, gain_ref, down_ref, ups_ref,
+UP_START = 1
+UP_PLACES = (0, 4, 8)
+
+
+def one_hot(rows, columns, first):
+    at = lax.broadcasted_iota(jnp.int32, (rows, columns), 0) + first
+    return (at == lax.broadcasted_iota(jnp.int32, (rows, columns), 1)).astype(BF)
+
+
+def down_maps(qd, vd):
+    rank = qd.shape[0]
+    return (dot(qd, one_hot(rank, 128, 0), TN) + dot(vd, one_hot(rank, 128, rank), TN)).astype(BF)
+
+
+def up_map(up, first):
+    return (ADAPTER_SCALE * dot(one_hot(up.shape[0], 128, first), up, TN)).astype(BF)
+
+
+def front_kernel(nb, ns, size, tile, layout, x_hbm, cot_hbm, wq_ref, wk_ref, wv_ref, wo_ref, up_hbm, gain_ref, qd_ref, qu_ref, vd_ref, vu_ref,
                  qkv_out, att_out, mixed_out, lse_ref, low_out, x_out, cot_out, wq_out, wk_out, wv_out, wo_out, up_out,
-                 xs, n1s, stage, qkv, att, lows, ws, own, send, recv, usend, urecv, xsend, xrecv, csend, crecv,
+                 xs, n1s, stage, qkv, att, lows, ws, own, down_ref, ups_ref, send, recv, usend, urecv, xsend, xrecv, csend, crecv,
                  osend, orecv, asend, arecv, local_sem, qkv_sem, att_sem):
     docs, rows, d = x_hbm.shape
     w = d // ns
@@ -333,11 +362,17 @@
                 steps[t - delays[n]]()
             if t == ready[n]:
                 keeps[n].start()
-        if t == ready[0] + 1:
+        if t == UP_START + ready[0]:
             fetch.wait()
             up_steps[0]()
 
-    for t in range(ready[0] + 1):
+    slot(0)
+    rank = qu_ref.shape[0]
+    down_ref[...] = down_maps(qd_ref[...], vd_ref[...])
+    ups_ref[0] = up_map(qu_ref[...], 0)
+    ups_ref[1] = jnp.zeros((128, d), BF)
+    ups_ref[2] = up_map(vu_ref[...], rank)
+    for t in range(1, ready[0] + 1):
         slot(t)
     places = {2 * docs - 5 + 2 * n: t for n, t in enumerate(range(ready[0] + 1, ready[3] + 1))}
 
@@ -368,11 +403,12 @@
             src_ref=att.at[flip(p.part, r), i], dst_ref=mixed_out.at[p.part, i], send_sem=asend.at[i, r],
             recv_sem=arecv.at[i, r], device_id=p.peer(r), device_id_type=MESH)
 
+    inside = [n for n in range(1, len(up_steps)) if n <= len(UP_PLACES) and UP_PLACES[n - 1] < docs * pairs]
+
     def one_pair(m, carry):
         doc, pair = m // pairs, m % pairs
-        for n in range(1, len(up_steps)):
-            if PACE * (n - 1) < docs * pairs:
-                pl.when(m == PACE * (n - 1))(up_steps[n])
+        for n in inside:
+            pl.when(m == UP_PLACES[n - 1])(up_steps[n])
 
         @pl.when(pair == 0)
         def _():
@@ -394,7 +430,7 @@
 
     lax.fori_loop(0, docs * pairs, one_pair, 0)
     for n in range(1, len(up_steps)):
-        if PACE * (n - 1) >= docs * pairs:
+        if n not in inside:
             up_steps[n]()
     for i in range(docs):
         x_keep(i).wait()
@@ -411,7 +447,7 @@
         g.drain()
 
 
-def front(nb, ns, layout, x, cot, wq, wk, wv, wo, up, gain, down, ups, size, tile=256):
+def front(nb, ns, layout, x, cot, wq, wk, wv, wo, up, gain, adapters, size, tile=256):
     docs, rows, d = x.shape
     w = d // ns
     n = rows * ns
@@ -424,18 +460,18 @@
             like(docs, rows, 128), like(*x.shape), like(*x.shape)] + [like(nb, *wq.shape)] * 4 + [like(nb, *up.shape)]
     return pl.pallas_call(
         functools.partial(front_kernel, nb, ns, size, tile),
-        in_specs=[pl.BlockSpec(memory_space=pltpu.SMEM)] + [any_spec] * 7 + [vmem] * 3,
+        in_specs=[pl.BlockSpec(memory_space=pltpu.SMEM)] + [any_spec] * 7 + [vmem] * 5,
         out_specs=[any_spec] * 3 + [vmem] + [any_spec] * 8,
         out_shape=outs,
         scratch_shapes=[pltpu.VMEM(x.shape, BF), pltpu.VMEM(x.shape, BF), pltpu.VMEM((3, docs, ns, rows, w), BF),
                         pltpu.VMEM((3,) + heads, BF), pltpu.VMEM(heads, BF), pltpu.VMEM((docs, rows, 128), BF),
                         pltpu.VMEM((4, nb) + wq.shape, BF), pltpu.VMEM(up.shape, BF),
-                        dma((4, 4, nb)), dma((4, nb)), dma((4, nb)), dma((nb,)), dma((docs,)), dma((docs,)),
+                        pltpu.VMEM((d, 128), BF), pltpu.VMEM((3, 128, d), BF), dma((4, 4, nb)), dma((4, nb)), dma((4, nb)), dma((nb,)), dma((docs,)), dma((docs,)),
                         dma((docs,)), dma((docs,)), dma((3, docs, ns)), dma((3, docs, ns)), dma((docs, ns)), dma((docs, ns)),
                         dma((docs + 6,)), dma((docs,)), dma((docs, 2))],
         compiler_params=pltpu.CompilerParams(collective_id=0, has_side_effects=True, vmem_limit_bytes=62 << 20),
         name="front",
-    )(layout, x, cot, wq, wk, wv, wo, up, gain, down, ups)
+    )(layout, x, cot, wq, wk, wv, wo, up, gain, *adapters)
 
 
 def middle_kernel(nb, ns, x_hbm, att_hbm, kept_hbm, cot_hbm, gain_ref, wo_hbm, up_hbm, down_hbm,
@@ -580,43 +616,54 @@
     )(x, att, kept, cot, gain, wo, up, down)
 
 
-def sum_over_devices(p, mine, first, second, total, sends, recvs):
-    b, s, nb, ns = p.b, p.s, p.nb, p.ns
-    slot, block = b % 16, b - b % 16
-    many = nb // 16 * ns
-    at = (b // 16) * ns + s
-
-    def scatter(j):
+class DeviceSum:
+    def __init__(self, p, mine, first, second, total, sends, recvs):
+        self.p, self.mine, self.first, self.second, self.total = p, mine, first, second, total
+        self.sends, self.recvs = sends, recvs
+        self.slot, self.block = p.b % 16, p.b - p.b % 16
+        self.many = p.nb // 16 * p.ns
+        self.at = (p.b // 16) * p.ns + p.s
+
+    def copy(self, phase, j, src, dst, device):
         return pltpu.make_async_remote_copy(
-            src_ref=mine.at[flip(slot, j)], dst_ref=first.at[slot], send_sem=sends.at[0, j], recv_sem=recvs.at[0, j],
-            device_id=(block + flip(slot, j), s), device_id_type=MESH)
-
-    def share(j):
-        to = flip(at, j)
-        return pltpu.make_async_remote_copy(
-            src_ref=second.at[at], dst_ref=second.at[at], send_sem=sends.at[1, j], recv_sem=recvs.at[1, j],
-            device_id=((to // ns) * 16 + slot, to % ns), device_id_type=MESH)
-
-    def spread(j):
-        return pltpu.make_async_remote_copy(
-            src_ref=total.at[slot], dst_ref=total.at[slot], send_sem=sends.at[2, j], recv_sem=recvs.at[2, j],
-            device_id=(block + flip(slot, j), s), device_id_type=MESH)
-
-    for j in range(1, 16):
-        scatter(j).start()
-    first[slot] = mine[slot]
-    for j in range(1, 16):
-        scatter(j).wait()
-    second[at] = jnp.sum(first[...], axis=0)
-    for j in range(1, many):
-        share(j).start()
-    for j in range(1, many):
-        share(j).wait()
-    total[slot] = jnp.sum(second[...], axis=0)
-    for j in range(1, 16):
-        spread(j).start()
-    for j in range(1, 16):
-        spread(j).wait()
+            src_ref=src, dst_ref=dst, send_sem=self.sends.at[phase, j], recv_sem=self.recvs.at[phase, j],
+            device_id=device, device_id_type=MESH)
+
+    def fellow(self, j):
+        return (self.block + flip(self.slot, j), self.p.s)
+
+    def scatter(self, j):
+        return self.copy(0, j, self.mine.at[flip(self.slot, j)], self.first.at[self.slot], self.fellow(j))
+
+    def share(self, j):
+        to, ns = flip(self.at, j), self.p.ns
+        return self.copy(1, j, self.second.at[self.at], self.second.at[self.at], ((to // ns) * 16 + self.slot, to % ns))
+
+    def spread(self, j):
+        return self.copy(2, j, self.total.at[self.slot], self.total.at[self.slot], self.fellow(j))
+
+    def begin(self):
+        for j in range(1, 16):
+            self.scatter(j).start()
+        self.first[self.slot] = self.mine[self.slot]
+
+    def middle(self):
+        for j in range(1, 16):
+            self.scatter(j).wait()
+        self.second[self.at] = jnp.sum(self.first[...], axis=0)
+        for j in range(1, self.many):
+            self.share(j).start()
+
+    def end(self):
+        for j in range(1, self.many):
+            self.share(j).wait()
+        self.total[self.slot] = jnp.sum(self.second[...], axis=0)
+        for j in range(1, 16):
+            self.spread(j).start()
+
+    def finish(self):
+        for j in range(1, 16):
+            self.spread(j).wait()
 
 
 def sum_ways(p):
@@ -634,8 +681,9 @@
 
 
 def backward_kernel(nb, ns, rank, size, tile, layout, q_ref, k_ref, v_ref, o_ref, g_ref, lse_ref, top_hbm, x_hbm, gain_ref,
-                    rg_hbm, low_hbm, wq_hbm, wk_hbm, wv_hbm, down_ref, upq_ref, upv_ref, top_out, out_hbm, sum_ref,
+                    rg_hbm, low_hbm, wq_hbm, wk_hbm, wv_hbm, qd_ref, qu_ref, vd_ref, vu_ref, top_out, out_hbm, sum_ref,
                     dqt, stage, xs, rgs, ds, wqs, wks, wvs, lows, outs, gds, gqs, gvs, mine, first, second, summed,
+                    tops, xhs, lgs, down_ref, upq_ref, upv_ref,
                     load, dsend, drecv, osend, orecv, tsend, trecv, ssend, srecv):
     docs, rows, d = x_hbm.shape
     w = d // ns
@@ -645,10 +693,11 @@
     loads = [pltpu.make_async_copy(a, v, load.at[n]) for n, (a, v) in enumerate(
         ((wq_hbm, wqs), (wk_hbm, wks), (wv_hbm, wvs), (low_hbm, lows), (x_hbm, xs), (rg_hbm, rgs)))]
 
-    def away(t, i, r):
+    def away(t, i, r, n):
+        at = pl.ds(pl.multiple_of(n * 128, 128), 128)
         return pltpu.make_async_remote_copy(
-            src_ref=stage.at[i, t, flip(p.part, r)], dst_ref=ds.at[t, p.part, i], send_sem=dsend.at[t, i, r],
-            recv_sem=drecv.at[t, i, r], device_id=p.peer(r), device_id_type=MESH)
+            src_ref=stage.at[i, t, flip(p.part, r), :, at], dst_ref=ds.at[t, p.part, i, :, at], send_sem=dsend.at[t, i, r, n],
+            recv_sem=drecv.at[t, i, r, n], device_id=p.peer(r), device_id_type=MESH)
 
     cut = rows // CUTS
 
@@ -667,18 +716,41 @@
             src_ref=top_hbm.at[i], dst_ref=top_out.at[i], send_sem=tsend.at[i], recv_sem=trecv.at[i],
             device_id=p.partner, device_id_type=MESH)
 
+    top_in = pltpu.make_async_copy(top_hbm, tops, tsend.at[0])
+    top_home = pltpu.make_async_copy(tops, top_out, trecv.at[0])
+    ways = [(p.peer(r), None) for r in range(1, ns)] + [(p.partner, jnp.logical_not(p.stays))] + sum_ways(p)
+    total = DeviceSum(p, mine, first, second, summed, ssend, srecv)
+
     @pl.when((doc == 0) & (pair == 0))
     def _():
+        p.hello(ways)
         for copy in loads:
             copy.start()
-        p.greet([(p.peer(r), None) for r in range(1, ns)] + [(p.partner, jnp.logical_not(p.stays))] + sum_ways(p))
-        for i in range(docs):
-            pl.when(jnp.logical_not(p.stays))(lambda i=i: top_away(i).start())
+        pl.when(p.stays)(lambda: top_in.start())
+        down_ref[...] = down_maps(qd_ref[...], vd_ref[...])
+        upq_ref[...] = up_map(qu_ref[...], 0)
+        upv_ref[...] = up_map(vu_ref[...], rank)
         gds[...] = jnp.zeros_like(gds)
         gqs[...] = jnp.zeros_like(gqs)
         gvs[...] = jnp.zeros_like(gvs)
 
-    @pl.when((doc > 0) & (pair == min(1, pairs - 1)))
+    @pl.when(doc < docs)
+    def _():
+        attention_gradients(layout, q_ref, k_ref, v_ref, o_ref, g_ref, lse_ref, stage, dqt, doc, pair, size, tile)
+
+        @pl.when((doc == 0) & (pair == 0))
+        def _():
+            p.met(ways)
+            pl.when(p.stays)(lambda: top_in.wait())
+            pl.when(p.stays)(lambda: top_home.start())
+            for i in range(docs):
+                pl.when(jnp.logical_not(p.stays))(lambda i=i: top_away(i).start())
+
+        for t in range(3):
+            for r in range(1, ns):
+                away(t, doc, r, pair).start()
+
+    @pl.when((doc > 0) & (pair == 0))
     def _():
         i = doc - 1
 
@@ -689,53 +761,55 @@
 
         for t in range(3):
             for r in range(1, ns):
-                away(t, i, r).wait()
+                for n in range(pairs):
+                    away(t, i, r, n).wait()
+
+        xh, inv = normalise(xs[i].astype(F32))
+        xhs[:, :d] = xh
+        xhs[:, d:] = jnp.broadcast_to(inv, (rows, 128))
+        lg = jnp.zeros((rows, 128), F32)
+        for r in range(ns):
+            g = flip(p.part, r)
+            cols = pl.ds(pl.multiple_of(g * w, w), w)
+            for t, up, grads in ((0, upq_ref, gqs), (2, upv_ref, gvs)):
+                piece = ds[t, g, i] if r else stage[i, t, p.part]
+                lg = lg + dot(piece, up[:, cols], NT)
+                grads[:, cols] += dot(lows[i], piece, TN)
+        lgs[...] = lg.astype(BF)
+        gds[...] += dot(lgs[...], (xh * gain_ref[...]).astype(BF), TN)
+
+        @pl.when(i == docs - 1)
+        def _():
+            upper = lax.broadcasted_iota(jnp.int32, (2 * rank, 1), 0) < rank
+            both = jnp.where(upper, gqs[:2 * rank, :], gvs[:2 * rank, :]) * ADAPTER_SCALE
+            for n in range(8):
+                mine[n] = gds[:8, n * 128:(n + 1) * 128]
+                mine[8 + n] = both[:, n * 128:(n + 1) * 128]
+            total.begin()
 
         def some_rows(n, carry):
             at = pl.ds(pl.multiple_of(n * cut, cut), cut)
-            low = lows[i, at, :]
-            fg = lg = None
+            fg = dot(lgs[at, :], down_ref[...], NT)
             for r in range(ns):
                 g = flip(p.part, r)
                 cols = pl.ds(pl.multiple_of(g * w, w), w)
-                for t, (full, up, total) in enumerate(((wqs, upq_ref, gqs), (wks, None, None), (wvs, upv_ref, gvs))):
+                for t, full in enumerate((wqs, wks, wvs)):
                     piece = ds[t, g, i, at, :] if r else stage[i, t, p.part, at, :]
-                    y = dot(piece, full[:, :, cols].reshape(d, w), NT)
-                    fg = y if fg is None else fg + y
-                    if up is not None:
-                        y = dot(piece, up[:, cols], NT)
-                        lg = y if lg is None else lg + y
-                        total[:, cols] += dot(low, piece, TN)
-            lgb = lg.astype(BF)
-            fg = fg + dot(lgb, down_ref[...], NT)
-            xh, inv = normalise(xs[i, at, :].astype(F32))
-            gds[...] += dot(lgb, (xh * gain_ref[...]).astype(BF), TN)
-            outs[i, at, :] = (rgs[i, at, :] + norm_back(xh, inv, gain_ref[...], fg)).astype(BF)
+                    fg = fg + dot(piece, full[:, :, cols].reshape(d, w), NT)
+            outs[i, at, :] = (rgs[i, at, :] + norm_back(xhs[at, :d], xhs[at, d:d + 1], gain_ref[...], fg)).astype(BF)
             pl.when(p.stays)(lambda: out_home(i, n).start())
             pl.when(jnp.logical_not(p.stays))(lambda: out_away(i, n).start())
+            pl.when((i == docs - 1) & (n == 0))(total.middle)
             return carry
 
         lax.fori_loop(0, CUTS, some_rows, 0)
-
-    @pl.when(doc < docs)
-    def _():
-        attention_gradients(layout, q_ref, k_ref, v_ref, o_ref, g_ref, lse_ref, stage, dqt, doc, pair, size, tile)
-
-        @pl.when(pair == pairs - 1)
-        def _():
-            for t in range(3):
-                for r in range(1, ns):
-                    away(t, doc, r).start()
+        pl.when(i == docs - 1)(total.end)
 
     @pl.when((doc == docs) & (pair == pairs - 1))
     def _():
-        upper = lax.broadcasted_iota(jnp.int32, (2 * rank, 1), 0) < rank
-        both = jnp.where(upper, gqs[:2 * rank, :], gvs[:2 * rank, :]) * ADAPTER_SCALE
-        for n in range(8):
-            mine[n] = gds[:8, n * 128:(n + 1) * 128]
-            mine[8 + n] = both[:, n * 128:(n + 1) * 128]
-        sum_over_devices(p, mine, first, second, summed, ssend, srecv)
+        total.finish()
         sum_ref[...] = summed[...]
+        pl.when(p.stays)(lambda: top_home.wait())
         for i in range(docs):
             for n in range(CUTS):
                 pl.when(p.stays)(lambda i=i, n=n: out_home(i, n).wait())
@@ -771,6 +845,25 @@
         lo, hi = j * tile, (j + 1) * tile
         return dot(k[lo:hi], qms[h][lo:], NT), dot(v[lo:hi], gms[h][lo:], NT)
 
+    waiting = []
+    sums = {}
+
+    def settle():
+        j, h, p, ds = waiting.pop(0)
+        lo, hi = j * tile, (j + 1) * tile
+        dv = dot(p, gms[h][lo:])
+        dk = dot(ds, qms[h][lo:])
+        dq = dot(kt[64 * h:64 * h + 64, lo:hi], ds)
+        if j == 0:
+            dqt[64 * h:64 * h + 64, :] = dq
+        else:
+            dqt[64 * h:64 * h + 64, lo:] += dq
+        if h == 0:
+            sums[j] = dk, dv
+        else:
+            dks.append(((sums[j][0] + dk) * SCORE_SCALE).astype(BF))
+            dvs.append((sums[j][1] + dv).astype(BF))
+
     ahead = products(*work[0])
     for t, (j, h) in enumerate(work):
         st, dp = ahead
@@ -780,19 +873,10 @@
         p = jnp.exp2(st * c - lse[h:h + 1, lo:])
         diag = jnp.where(tri, p[:, :tile], 0.0)
         p = diag if hi == n else jnp.concatenate([diag, p[:, tile:]], axis=1)
-        ds = (p * (dp - delta[h:h + 1, lo:])).astype(BF)
-        dvh = dot(p.astype(BF), gms[h][lo:])
-        dkh = dot(ds, qms[h][lo:])
-        dv = dvh if h == 0 else dv + dvh
-        dk = dkh if h == 0 else dk + dkh
-        dqh = dot(kt[64 * h:64 * h + 64, lo:hi], ds)
-        if j == 0:
-            dqt[64 * h:64 * h + 64, :] = dqh
-        else:
-            dqt[64 * h:64 * h + 64, lo:] += dqh
-        if h == 1:
-            dks.append((dk * SCORE_SCALE).astype(BF))
-            dvs.append(dv.astype(BF))
+        waiting.append((j, h, p.astype(BF), (p * (dp - delta[h:h + 1, lo:])).astype(BF)))
+        if t:
+            settle()
+    settle()
     lanes = pl.ds(pl.multiple_of(pair * 128, 128), 128)
     for t, value in enumerate(((dqt[...] * SCORE_SCALE).T.astype(BF), jnp.concatenate(dks, axis=0),
                                jnp.concatenate(dvs, axis=0))):
@@ -801,7 +885,7 @@
         put_back(value, layout, blocks, size, store)
 
 
-def backward(nb, ns, rank, layout, qkv, o, g, lse, top, x, gain, rg, low, wq, wk, wv, down, upq, upv, size, tile=256):
+def backward(nb, ns, rank, layout, qkv, o, g, lse, top, x, gain, rg, low, wq, wk, wv, adapters, size, tile=256):
     docs, rows, d = x.shape
     parts = o.shape[0]
     w = d // ns
@@ -821,7 +905,7 @@
         grid=(docs + 1, w // 128),
         in_specs=[pl.BlockSpec(memory_space=pltpu.SMEM), third(0), third(1), third(2), spec, spec]
         + [pl.BlockSpec((1, 1, 2, n), lambda i, j: (jnp.minimum(i, docs - 1), j, 0, 0))]
-        + [any_spec] * 2 + [vmem] + [any_spec] * 5 + [vmem] * 3,
+        + [any_spec] * 2 + [vmem] + [any_spec] * 5 + [vmem] * 4,
         out_specs=[any_spec, any_spec, vmem],
         out_shape=[row, row, jax.ShapeDtypeStruct((16, 8, 128), F32)],
         scratch_shapes=[pltpu.VMEM((128, n), F32), pltpu.VMEM((docs, 3, parts, rows, w), BF),
@@ -830,11 +914,13 @@
         + [pltpu.VMEM(low.shape, BF), pltpu.VMEM(x.shape, BF)] + [pltpu.VMEM((128, d), F32)] * 3
         + [pltpu.VMEM((16, 8, 128), F32), pltpu.VMEM((16, 8, 128), F32), pltpu.VMEM((nb // 16 * ns, 8, 128), F32),
            pltpu.VMEM((16, 8, 128), F32),
-           dma((6,)), dma((3, docs, ns)), dma((3, docs, ns)), dma((docs, CUTS)), dma((docs, CUTS)), dma((docs,)), dma((docs,)),
+           pltpu.VMEM(x.shape, BF), pltpu.VMEM((rows, d + 128), F32), pltpu.VMEM((rows, 128), BF),
+           pltpu.VMEM((d, 128), BF), pltpu.VMEM((128, d), BF), pltpu.VMEM((128, d), BF),
+           dma((6,)), dma((3, docs, ns, w // 128)), dma((3, docs, ns, w // 128)), dma((docs, CUTS)), dma((docs, CUTS)), dma((docs,)), dma((docs,)),
            dma((3, many)), dma((3, many))],
         compiler_params=pltpu.CompilerParams(collective_id=3, has_side_effects=True, vmem_limit_bytes=62 << 20),
         name="backward",
-    )(layout, qkv, qkv, qkv, o, g, lse, top, x, gain, rg, low, wq, wk, wv, down, upq, upv)
+    )(layout, qkv, qkv, qkv, o, g, lse, top, x, gain, rg, low, wq, wk, wv, *adapters)
 
 
 def local(
@@ -846,20 +932,16 @@
     docs, rows, d = tokens.shape
     size = rows * ns // layout.shape[0]
     rank = query_up_adapter.shape[0]
-    down = jnp.pad(jnp.concatenate([query_down_adapter, value_down_adapter], axis=1), ((0, 0), (0, 128 - 2 * rank)))
-    upq = jnp.pad((ADAPTER_SCALE * query_up_adapter).astype(BF), ((0, 128 - rank), (0, 0)))
-    upv = jnp.pad((ADAPTER_SCALE * value_up_adapter).astype(BF), ((rank, 128 - 2 * rank), (0, 0)))
+    adapters = (query_down_adapter.T, query_up_adapter, value_down_adapter.T, value_up_adapter)
     gain1 = attention_norm_gain[None]
     gain2 = feedforward_norm_gain[None]
 
     qkv, att, mixed, lse, low, x, cot, wq, wk, wv, wo, w_up = front(
         nb, ns, layout, tokens, cotangent, query_weight, key_weight, value_weight, attention_output_weight, up_weight,
-        gain1, down, jnp.stack([upq, jnp.zeros_like(upq), upv]), size)
+        gain1, adapters, size)
     out, rg, mix = middle(nb, ns, x, mixed, cotangent, cot, gain2, wo.reshape(d, d), w_up, down_weight)
-    stays = lax.axis_index("batch") % 2 == lax.axis_index("seq") % 2
-    got, input_grad, sums = backward(
-        nb, ns, rank, layout, qkv, att, mix, lse, out, x, gain1, rg, low, wq, wk, wv, down, upq, upv, size)
-    layer_out = jnp.where(stays, out, got)
+    layer_out, input_grad, sums = backward(
+        nb, ns, rank, layout, qkv, att, mix, lse, out, x, gain1, rg, low, wq, wk, wv, adapters, size)
     sums = sums.reshape(2, d // 128, 2 * rank, 128).transpose(0, 2, 1, 3).reshape(2, 2 * rank, d)
     return (layer_out, input_grad, sums[0, :rank].T, sums[1, :rank], sums[0, rank:].T, sums[1, rank:])
 

time: 304 us -> 292 us (0.961)
  other arithmetic: 7.19 us -> 0 us
  Pallas kernels: 291 us -> 284 us
    pallas_call x1, Pallas kernels: 91.8 us -> 86.8 us  [backward(): pl.pallas_call(functools.partial(backward_kernel, nb, ns, rank, size, til...]
    select_n x1 -> x0, other arithmetic: 4.04 us -> none  [local(): layer_out = jnp.where(stays, out, got)]
    unnamed x5 -> x4, local copies, waits for them, and re-layouts: 1.67 us -> 5.68 us
where the time goes in v3:
time: 292 us; the launch traced here: 291 us
  Pallas kernels  284 us (97%)
  local copies, waits for them, and re-layouts  7.16 us (2%)
    pallas_call x1, Pallas kernels, front(): pl.pallas_call(functools.partial(front_kernel, nb, ns, size, tile), in_sp...  110 us
    pallas_call x1, Pallas kernels, backward(): pl.pallas_call(functools.partial(backward_kernel, nb, ns, rank, size, til...  86.8 us
    pallas_call x1, Pallas kernels, middle(): pl.pallas_call(functools.partial(middle_kernel, nb, ns), in_specs=[any_sp...  86.5 us

profile of v3, /device:TPU:1, one launch (start us, length us, event | category | flops | bytes accessed | tf_op | source)
XLA Modules:
  0.0 291.4 jit_solution(9467334065604846363)
XLA Ops:
  0.6 110.3 %front.1 = (bf16[3,2,3,512,512]{4,3,2,1,0:T(8,128)(2,1)}, bf16[2,3,512,512]{3,2,1,0:T(8,128)(2,1)}, bf16[2,3,512,512]{3,2,1,0:T(8,128)(2,1)}, f32[3,4,2,1024]{3,...) custom-call(s32[4]{0:T(128)} %layout.3, ...), custom_call_target="tpu_custom_call" | custom-call | tf_op jit(solution)/shard_map/front/pallas_call | solution.py:461
  111.0 86.5 %feed_forward.1 = (bf16[3,512,1024]{2,1,0:T(8,128)(2,1)}, f32[3,512,1024]{2,1,0:T(8,128)}, bf16[2,3,512,512]{3,2,1,0:T(8,128)(2,1)}) custom-call(bf16[3,512,1024]{2,1,0:T(8,128)(2,1)} %get-tuple-element.26.x_hbm, bf16[2,3,512,512]{3,2,1,0:T(8,128)(2,1)} %get-tuple-element.27.att_hbm, bf16[3,512,1024]{2,1,0:T(8,128)(2,1)} %kept_hbm.1, ...), custom_call_target="tpu_custom_call" | custom-call | tf_op jit(solution)/shard_map/feed_forward/pallas_call | solution.py:601
  197.4 86.8 %backward.1 = (bf16[3,512,1024]{2,1,0:T(8,128)(2,1)}, bf16[3,512,1024]{2,1,0:T(8,128)(2,1)}, f32[16,8,128]{2,1,0:T(8,128)}) custom-call(s32[4]{0:T(128)} %layout.3, bf16[3,2,3,512,512]{4,3,2,1,0:T(8,128)(2,1)} %get-tuple-element.24.q_ref.k_ref.v_ref, bf16[3,2,3,512,512]{4,3,2,1,0:T(8,128)(2,1)} %get-tuple-element.24.q_ref.k_ref.v_ref, ...), custom_call_target="tpu_custom_call" | custom-call | tf_op jit(solution)/shard_map/backward/pallas_call | solution.py:903
  284.3 1.5 slice_bitcast_fusion
  285.7 0.0 copy-start
  285.7 4.0 %copy.23 = bf16[3,512,1024]{2,1,0:T(8,128)(2,1)} copy(bf16[3,512,1024]{2,1,0:T(8,128)(2,1)} %get-tuple-element.52) | data formatting | bytes 6291456
  289.7 0.0 copy-done
  289.7 1.7 copy.24
Async XLA Ops:
  285.7 4.0 %copy-start = (bf16[3,512,1024]{2,1,0:T(8,128)(2,1)S(1)}, bf16[3,512,1024]{2,1,0:T(8,128)(2,1)}, u32[]{:S(2)}) copy-start(bf16[3,512,1024]{2,1,0:T(8,128)(2,1)} %get-tuple-element.53) | copy-start | bytes 9437188

commit v4 on v3

--- a/solution.py
+++ b/solution.py
@@ -119,9 +119,15 @@
         p = self.p
         pl.when(p.line + 1 < p.lines)(lambda: self.copy(p.b, 0, self.own).start())
         pl.when(p.line > 0)(lambda: self.copy(p.b, 1, self.own).start())
-        self.copy(p.b, 2, self.own).start()
+        self.hand_pair(p.line, self.own)
         self.copy(p.b, 3, self.own).start()
         self.mine().start()
+
+    def hand_pair(self, line, src=None):
+        self.copy(self.part(line), 2, src).start()
+
+    def pair_sent(self, line):
+        self.copy(self.part(line), 2).wait_send()
 
     def hop(self, k, pairs=True):
         p = self.p
@@ -132,15 +138,12 @@
             more = p.line + 1 < p.lines if way == 0 else p.line > 0
             pl.when(more)(lambda: self.copy(i, way).start())
             if pairs:
-                self.copy(i, 2).start()
+                self.hand_pair(line)
             self.copy(i, 3).start()
 
         below, above = p.line - k, p.line + k
         pl.when(below >= 0)(lambda: take(0, below))
         pl.when(above < p.lines)(lambda: take(1, above))
-
-    def pair_line(self, line):
-        self.copy(self.part(line), 2).start()
 
     def relay_line(self, line):
         i = self.part(line, 1)
@@ -170,7 +173,7 @@
             i = self.part(line)
             pl.when((p.line >= line) & (p.line + 1 < p.lines))(lambda i=i: self.copy(i, 0).wait_send())
             pl.when((p.line <= line) & (p.line > 0))(lambda i=i: self.copy(i, 1).wait_send())
-            self.copy(i, 2).wait_send()
+            self.pair_sent(line)
             self.copy(i, 3).wait_send()
             self.copy(self.part(line, 1), 3).wait_send()
 
@@ -181,6 +184,46 @@
         out.append(functools.partial(self.relay, self.p.lines - 1))
         out.append(self.finish)
         return out
+
+
+class PlaneGather(Gather):
+    def __init__(self, place, own, full, send, recv):
+        super().__init__(place, own, full, send, recv)
+        self.lacks = flip(place.line, 1 + place.s % 2)
+        self.gives = flip(place.line, 2 - place.s % 2)
+
+    def to_plane(self, i):
+        p = self.p
+        return pltpu.make_async_remote_copy(
+            src_ref=self.full.at[i], dst_ref=self.full.at[i], send_sem=self.send.at[4, i], recv_sem=self.recv.at[i],
+            device_id=(p.b, flip(p.s, 1)), device_id_type=MESH)
+
+    def hand_pair(self, line, src=None):
+        pl.when(line != self.lacks)(lambda: super(PlaneGather, self).hand_pair(line, src))
+
+    def pair_sent(self, line):
+        pl.when(line != self.lacks)(lambda: super(PlaneGather, self).pair_sent(line))
+
+    def relay_line(self, line):
+        @pl.when(line != self.lacks)
+        def _():
+            i = self.part(line, 1)
+            self.copy(i, 2).wait_recv()
+            pl.when(line == self.gives)(lambda: self.to_plane(i).start())
+            self.copy(i, 3).start()
+
+    def cross(self):
+        i = self.part(self.lacks, 1)
+        self.to_plane(i).wait_recv()
+        self.copy(i, 3).start()
+
+    def drain(self):
+        super().drain()
+        self.to_plane(self.part(self.gives, 1)).wait_send()
+
+    def steps(self):
+        out = super().steps()
+        return out[:-1] + [self.cross] + out[-1:]
 
 
 def run(calls):
@@ -290,7 +333,8 @@
     p = Place(nb, ns)
     fetch = pltpu.make_async_copy(up_hbm, own, local_sem.at[docs + 5])
     fetch.start()
-    p.greet(p.gather_ways() + [(p.partner, jnp.logical_not(p.stays))] + [(p.peer(r), None) for r in range(1, ns)])
+    p.greet(p.gather_ways() + [((p.b, flip(p.s, 1)), None), (p.partner, jnp.logical_not(p.stays))]
+            + [(p.peer(r), None) for r in range(1, ns)])
 
     def x_remote(i):
         return pltpu.make_async_remote_copy(
@@ -350,7 +394,8 @@
     keeps = [pltpu.make_async_copy(ws.at[n], out, local_sem.at[docs + n])
              for n, out in enumerate((wq_out, wk_out, wv_out, wo_out))]
     low_keep = pltpu.make_async_copy(lows, low_out, local_sem.at[docs + 4])
-    up_steps = Gather(p, own, up_out, usend, urecv).steps()
+    up_gather = PlaneGather(p, own, up_out, usend, urecv)
+    up_steps = up_gather.steps()
 
     lists = [g.steps() for g in gathers]
     delays = (0, 0, 2, 4)
@@ -443,7 +488,7 @@
     for keep in keeps:
         keep.wait()
     low_keep.wait()
-    for g in gathers + [Gather(p, own, up_out, usend, urecv)]:
+    for g in gathers + [up_gather]:
         g.drain()
 
 
@@ -466,7 +511,7 @@
         scratch_shapes=[pltpu.VMEM(x.shape, BF), pltpu.VMEM(x.shape, BF), pltpu.VMEM((3, docs, ns, rows, w), BF),
                         pltpu.VMEM((3,) + heads, BF), pltpu.VMEM(heads, BF), pltpu.VMEM((docs, rows, 128), BF),
                         pltpu.VMEM((4, nb) + wq.shape, BF), pltpu.VMEM(up.shape, BF),
-                        pltpu.VMEM((d, 128), BF), pltpu.VMEM((3, 128, d), BF), dma((4, 4, nb)), dma((4, nb)), dma((4, nb)), dma((nb,)), dma((docs,)), dma((docs,)),
+                        pltpu.VMEM((d, 128), BF), pltpu.VMEM((3, 128, d), BF), dma((4, 4, nb)), dma((4, nb)), dma((5, nb)), dma((nb,)), dma((docs,)), dma((docs,)),
                         dma((docs,)), dma((docs,)), dma((3, docs, ns)), dma((3, docs, ns)), dma((docs, ns)), dma((docs, ns)),
                         dma((docs + 6,)), dma((docs,)), dma((docs, 2))],
         compiler_params=pltpu.CompilerParams(collective_id=0, has_side_effects=True, vmem_limit_bytes=62 << 20),
@@ -545,7 +590,7 @@
             @pl.when((i == docs - 1) & (f % 2 == 0))
             def _():
                 pl.when(f // 2 + 1 < p.lines)(lambda: gather.hop(f // 2 + 1, pairs=False))
-                pl.when(f // 2 + 1 < p.lines)(lambda: gather.pair_line(flip(p.line, f // 2 + 1)))
+                pl.when(f // 2 + 1 < p.lines)(lambda: gather.hand_pair(flip(p.line, f // 2 + 1)))
 
             pl.when((i == min(1, docs - 1)) & (f % 2 == 0))(lambda: gather.relay_line(flip(p.line, f // 2)))
 

time: 292 us -> 290 us (level)
    pallas_call x1, Pallas kernels: 86.5 us -> 83.4 us  [middle(): pl.pallas_call(functools.partial(middle_kernel, nb, ns), in_specs=[any_sp...]
    pallas_call x1, Pallas kernels: 86.8 us -> 89.7 us  [backward(): pl.pallas_call(functools.partial(backward_kernel, nb, ns, rank, size, til...]
where the time goes in v4:
time: 290 us
  Pallas kernels  282 us (97%)
  local copies, waits for them, and re-layouts  7.16 us (2%)
    pallas_call x1, Pallas kernels, front(): pl.pallas_call(functools.partial(front_kernel, nb, ns, size, tile), in_sp...  109 us
    pallas_call x1, Pallas kernels, backward(): pl.pallas_call(functools.partial(backward_kernel, nb, ns, rank, size, til...  89.7 us
    pallas_call x1, Pallas kernels, middle(): pl.pallas_call(functools.partial(middle_kernel, nb, ns), in_specs=[any_sp...  83.4 us

profile of v4, /device:TPU:1, one launch (start us, length us, event | category | flops | bytes accessed | tf_op | source)
XLA Modules:
  0.0 289.7 jit_solution(5821260920072239445)
XLA Ops:
  0.6 108.7 %front.1 = (bf16[3,2,3,512,512]{4,3,2,1,0:T(8,128)(2,1)}, bf16[2,3,512,512]{3,2,1,0:T(8,128)(2,1)}, bf16[2,3,512,512]{3,2,1,0:T(8,128)(2,1)}, f32[3,4,2,1024]{3,...) custom-call(s32[4]{0:T(128)} %layout.3, ...), custom_call_target="tpu_custom_call" | custom-call | tf_op jit(solution)/shard_map/front/pallas_call | solution.py:506
  109.4 83.4 %feed_forward.1 = (bf16[3,512,1024]{2,1,0:T(8,128)(2,1)}, f32[3,512,1024]{2,1,0:T(8,128)}, bf16[2,3,512,512]{3,2,1,0:T(8,128)(2,1)}) custom-call(bf16[3,512,1024]{2,1,0:T(8,128)(2,1)} %get-tuple-element.26.x_hbm, bf16[2,3,512,512]{3,2,1,0:T(8,128)(2,1)} %get-tuple-element.27.att_hbm, bf16[3,512,1024]{2,1,0:T(8,128)(2,1)} %kept_hbm.1, ...), custom_call_target="tpu_custom_call" | custom-call | tf_op jit(solution)/shard_map/feed_forward/pallas_call | solution.py:646
  192.8 89.7 %backward.1 = (bf16[3,512,1024]{2,1,0:T(8,128)(2,1)}, bf16[3,512,1024]{2,1,0:T(8,128)(2,1)}, f32[16,8,128]{2,1,0:T(8,128)}) custom-call(s32[4]{0:T(128)} %layout.3, bf16[3,2,3,512,512]{4,3,2,1,0:T(8,128)(2,1)} %get-tuple-element.24.q_ref.k_ref.v_ref, bf16[3,2,3,512,512]{4,3,2,1,0:T(8,128)(2,1)} %get-tuple-element.24.q_ref.k_ref.v_ref, ...), custom_call_target="tpu_custom_call" | custom-call | tf_op jit(solution)/shard_map/backward/pallas_call | solution.py:948
  282.6 1.5 slice_bitcast_fusion
  284.1 0.0 copy-start
  284.1 4.0 %copy.23 = bf16[3,512,1024]{2,1,0:T(8,128)(2,1)} copy(bf16[3,512,1024]{2,1,0:T(8,128)(2,1)} %get-tuple-element.52) | data formatting | bytes 6291456
  288.1 0.0 copy-done
  288.1 1.7 copy.24
Async XLA Ops:
  284.1 4.0 %copy-start = (bf16[3,512,1024]{2,1,0:T(8,128)(2,1)S(1)}, bf16[3,512,1024]{2,1,0:T(8,128)(2,1)}, u32[]{:S(2)}) copy-start(bf16[3,512,1024]{2,1,0:T(8,128)(2,1)} %get-tuple-element.53) | copy-start | bytes 9437188

commit v5 on v4

--- a/solution.py
+++ b/solution.py
@@ -574,43 +574,48 @@
         up = ups[:, :, pl.ds(pl.multiple_of(base * held, chunk), chunk)].reshape(d, chunk)
         return up, downs[pl.ds(base, 2)].reshape(chunk, d)
 
+    tall = docs * rows // 2
+    tiles = nb // 2 * 2
+
+    def tile_of(t):
+        return pl.ds(pl.multiple_of(t % 2 * tall, tall), tall)
+
     def hidden(t):
-        up, down = weights(t // docs)
-        us[t % 2] = dot(n2s[rows_of(t % docs), :], up)
-        gs[t % 2] = dot(cots[t % docs], down, NT)
+        up, down = weights(t // 2)
+        us[t % 2] = dot(n2s[tile_of(t), :], up)
+        gs[t % 2] = dot(cots[tile_of(t), :], down, NT)
 
     def one_tile(t, carry):
-        f, i = t // docs, t % docs
-
-        @pl.when(t + 1 < nb // 2 * docs)
+        f, i = t // 2, t % 2
+        k, after = f // 2, f + 1
+
+        @pl.when((i == 0) & (f % 2 == 0))
         def _():
-            after = (t + 1) // docs
-            pl.when(i == docs - 1)(lambda: gather.from_core(flip(p.line, after // 2), after % 2))
-
-            @pl.when((i == docs - 1) & (f % 2 == 0))
+            @pl.when(k + 1 < p.lines)
             def _():
-                pl.when(f // 2 + 1 < p.lines)(lambda: gather.hop(f // 2 + 1, pairs=False))
-                pl.when(f // 2 + 1 < p.lines)(lambda: gather.hand_pair(flip(p.line, f // 2 + 1)))
-
-            pl.when((i == min(1, docs - 1)) & (f % 2 == 0))(lambda: gather.relay_line(flip(p.line, f // 2)))
-
-        hidden(jnp.minimum(t + 1, nb // 2 * docs - 1))
+                gather.hop(k + 1, pairs=False)
+                gather.hand_pair(flip(p.line, k + 1))
+
+            gather.relay_line(flip(p.line, k))
+
+        pl.when((i == 1) & (t + 1 < tiles))(lambda: gather.from_core(flip(p.line, after // 2), after % 2))
+        hidden(jnp.minimum(t + 1, tiles - 1))
         up, down = weights(f)
         act, slope = gelu_parts(us[t % 2])
         pg = (slope * gs[t % 2]).astype(BF)
-        at = rows_of(i)
+        at = tile_of(t)
         acc[at, :] += dot(act.astype(BF), down)
         dn[at, :] += dot(pg, up, NT)
         return carry
 
     gather.from_core(p.line, 0)
     hidden(0)
-    lax.fori_loop(0, nb // 2 * docs, one_tile, 0)
+    lax.fori_loop(0, tiles, one_tile, 0)
 
     def out_and_grad(i, carry):
         at = rows_of(i)
         xs[i] = acc[at, :].astype(BF)
-        rg = cots[i].astype(F32) + norm_back(xhs[at, :], invs[at, :1], gain_ref[...], dn[at, :])
+        rg = cots[at, :].astype(F32) + norm_back(xhs[at, :], invs[at, :1], gain_ref[...], dn[at, :])
         xhs[at, :] = rg
         mix = dot(rg.astype(BF), wos[...], NT).astype(BF)
         for g in range(ns):
@@ -650,15 +655,15 @@
         out_shape=[jax.ShapeDtypeStruct((docs, rows, d), BF), jax.ShapeDtypeStruct((docs, rows, d), F32),
                    jax.ShapeDtypeStruct((ns, docs, rows, w), BF)],
         scratch_shapes=[pltpu.VMEM((docs, rows, d), BF), pltpu.VMEM((ns, docs, rows, w), BF),
-                        pltpu.VMEM((docs, rows, d), BF), pltpu.VMEM(wo.shape, BF), pltpu.VMEM((nb,) + down.shape, BF),
+                        pltpu.VMEM((n, d), BF), pltpu.VMEM(wo.shape, BF), pltpu.VMEM((nb,) + down.shape, BF),
                         pltpu.VMEM(up.shape, BF), pltpu.VMEM((n, d), F32),
                         pltpu.VMEM((n, d), F32), pltpu.VMEM((n, d), F32), pltpu.VMEM((n, d), BF),
-                        pltpu.VMEM((n, 128), F32), pltpu.VMEM((2, rows, 2 * down.shape[0]), F32),
-                        pltpu.VMEM((2, rows, 2 * down.shape[0]), F32),
+                        pltpu.VMEM((n, 128), F32), pltpu.VMEM((2, n // 2, 2 * down.shape[0]), F32),
+                        pltpu.VMEM((2, n // 2, 2 * down.shape[0]), F32),
                         dma((4, nb)), dma((nb,)), dma((docs, ns)), dma((docs, ns)), dma((4 + docs,)), dma((3, docs))],
         compiler_params=pltpu.CompilerParams(collective_id=2, has_side_effects=True, vmem_limit_bytes=63 << 20),
         name="feed_forward",
-    )(x, att, kept, cot, gain, wo, up, down)
+    )(x, att, kept.reshape(n, d), cot.reshape(n, d), gain, wo, up, down)
 
 
 class DeviceSum:

time: 290 us -> 289 us (level)
  no operation moved by 1% of the time
where the time goes in v5:
time: 289 us
  Pallas kernels  281 us (97%)
  local copies, waits for them, and re-layouts  7.16 us (2%)
    pallas_call x1, Pallas kernels, front(): pl.pallas_call(functools.partial(front_kernel, nb, ns, size, tile), in_sp...  109 us
    pallas_call x1, Pallas kernels, backward(): pl.pallas_call(functools.partial(backward_kernel, nb, ns, rank, size, til...  89.7 us
    pallas_call x1, Pallas kernels, middle(): pl.pallas_call(functools.partial(middle_kernel, nb, ns), in_specs=[any_sp...  82.6 us

profile of v5, /device:TPU:1, one launch (start us, length us, event | category | flops | bytes accessed | tf_op | source)
XLA Modules:
  0.0 288.9 jit_solution(6659536544036693655)
XLA Ops:
  0.6 108.7 %front.1 = (bf16[3,2,3,512,512]{4,3,2,1,0:T(8,128)(2,1)}, bf16[2,3,512,512]{3,2,1,0:T(8,128)(2,1)}, bf16[2,3,512,512]{3,2,1,0:T(8,128)(2,1)}, f32[3,4,2,1024]{3,...) custom-call(s32[4]{0:T(128)} %layout.3, ...), custom_call_target="tpu_custom_call" | custom-call | tf_op jit(solution)/shard_map/front/pallas_call | solution.py:506
  109.4 82.6 %feed_forward.1 = (bf16[3,512,1024]{2,1,0:T(8,128)(2,1)}, f32[3,512,1024]{2,1,0:T(8,128)}, bf16[2,3,512,512]{3,2,1,0:T(8,128)(2,1)}) custom-call(bf16[3,512,1024]{2,1,0:T(8,128)(2,1)} %get-tuple-element.26.x_hbm, bf16[2,3,512,512]{3,2,1,0:T(8,128)(2,1)} %get-tuple-element.27.att_hbm, bf16[1536,1024]{1,0:T(8,128)(2,1)} %bitcast.24, ...), custom_call_target="tpu_custom_call" | custom-call | tf_op jit(solution)/shard_map/feed_forward/pallas_call | solution.py:651
  192.0 89.7 %backward.1 = (bf16[3,512,1024]{2,1,0:T(8,128)(2,1)}, bf16[3,512,1024]{2,1,0:T(8,128)(2,1)}, f32[16,8,128]{2,1,0:T(8,128)}) custom-call(s32[4]{0:T(128)} %layout.3, bf16[3,2,3,512,512]{4,3,2,1,0:T(8,128)(2,1)} %get-tuple-element.24.q_ref.k_ref.v_ref, bf16[3,2,3,512,512]{4,3,2,1,0:T(8,128)(2,1)} %get-tuple-element.24.q_ref.k_ref.v_ref, ...), custom_call_target="tpu_custom_call" | custom-call | tf_op jit(solution)/shard_map/backward/pallas_call | solution.py:953
  281.8 1.5 slice_bitcast_fusion
  283.2 0.0 copy-start
  283.2 4.0 %copy.23 = bf16[3,512,1024]{2,1,0:T(8,128)(2,1)} copy(bf16[3,512,1024]{2,1,0:T(8,128)(2,1)} %get-tuple-element.52) | data formatting | bytes 6291456
  287.2 0.0 copy-done
  287.2 1.7 copy.24
Async XLA Ops:
  283.2 4.0 %copy-start = (bf16[3,512,1024]{2,1,0:T(8,128)(2,1)S(1)}, bf16[3,512,1024]{2,1,0:T(8,128)(2,1)}, u32[]{:S(2)}) copy-start(bf16[3,512,1024]{2,1,0:T(8,128)(2,1)} %get-tuple-element.53) | copy-start | bytes 9437188

commit v6 on v5

--- a/solution.py
+++ b/solution.py
@@ -973,6 +973,25 @@
     )(layout, qkv, qkv, qkv, o, g, lse, top, x, gain, rg, low, wq, wk, wv, *adapters)
 
 
+def hand_out_kernel(a_ref, b_ref, a_out, b_out):
+    a_out[...] = a_ref[...]
+    b_out[...] = b_ref[...]
+
+
+def hand_out(a, b):
+    docs, rows, d = a.shape
+    cut = min(rows, 256)
+    spec = pl.BlockSpec((1, cut, d), lambda i, j: (i, j, 0))
+    return pl.pallas_call(
+        hand_out_kernel,
+        grid=(docs, rows // cut),
+        in_specs=[spec, spec],
+        out_specs=[spec, spec],
+        out_shape=[jax.ShapeDtypeStruct(a.shape, a.dtype), jax.ShapeDtypeStruct(b.shape, b.dtype)],
+        name="hand_out",
+    )(a, b)
+
+
 def local(
     nb, ns,
     tokens, cotangent, layout, attention_norm_gain, feedforward_norm_gain,
@@ -992,6 +1011,7 @@
     out, rg, mix = middle(nb, ns, x, mixed, cotangent, cot, gain2, wo.reshape(d, d), w_up, down_weight)
     layer_out, input_grad, sums = backward(
         nb, ns, rank, layout, qkv, att, mix, lse, out, x, gain1, rg, low, wq, wk, wv, adapters, size)
+    layer_out, input_grad = hand_out(layer_out, input_grad)
     sums = sums.reshape(2, d // 128, 2 * rank, 128).transpose(0, 2, 1, 3).reshape(2, 2 * rank, d)
     return (layer_out, input_grad, sums[0, :rank].T, sums[1, :rank], sums[0, rank:].T, sums[1, rank:])
 

time: 289 us -> 290 us (level)
  Pallas kernels: 281 us -> 288 us
  local copies, waits for them, and re-layouts: 7.16 us -> 0.64 us
    pallas_call x0 -> x1, Pallas kernels: none -> 6.81 us  [hand_out(): pl.pallas_call(hand_out_kernel, grid=(docs, rows // cut), in_specs=[spec,...]
    unnamed x4 -> x2, local copies, waits for them, and re-layouts: 5.68 us -> 0.01 us
where the time goes in v6:
time: 290 us; the launch traced here: 289 us
  Pallas kernels  288 us (99%)
    pallas_call x1, Pallas kernels, front(): pl.pallas_call(functools.partial(front_kernel, nb, ns, size, tile), in_sp...  109 us
    pallas_call x1, Pallas kernels, backward(): pl.pallas_call(functools.partial(backward_kernel, nb, ns, rank, size, til...  89.7 us
    pallas_call x1, Pallas kernels, middle(): pl.pallas_call(functools.partial(middle_kernel, nb, ns), in_specs=[any_sp...  82.6 us
    pallas_call x1, Pallas kernels, hand_out(): pl.pallas_call(hand_out_kernel, grid=(docs, rows // cut), in_specs=[spec,...  6.81 us

profile of v6, /device:TPU:1, one launch (start us, length us, event | category | flops | bytes accessed | tf_op | source)
XLA Modules:
  0.0 289.2 jit_solution(12473041639928701617)
XLA Ops:
  0.6 108.7 %front.1 = (bf16[3,2,3,512,512]{4,3,2,1,0:T(8,128)(2,1)}, bf16[2,3,512,512]{3,2,1,0:T(8,128)(2,1)}, bf16[2,3,512,512]{3,2,1,0:T(8,128)(2,1)}, f32[3,4,2,1024]{3,...) custom-call(s32[4]{0:T(128)} %layout.3, ...), custom_call_target="tpu_custom_call" | custom-call | tf_op jit(solution)/shard_map/front/pallas_call | solution.py:506
  109.4 82.6 %feed_forward.1 = (bf16[3,512,1024]{2,1,0:T(8,128)(2,1)}, f32[3,512,1024]{2,1,0:T(8,128)}, bf16[2,3,512,512]{3,2,1,0:T(8,128)(2,1)}) custom-call(bf16[3,512,1024]{2,1,0:T(8,128)(2,1)} %get-tuple-element.28.x_hbm, bf16[2,3,512,512]{3,2,1,0:T(8,128)(2,1)} %get-tuple-element.29.att_hbm, bf16[1536,1024]{1,0:T(8,128)(2,1)} %bitcast.24, ...), custom_call_target="tpu_custom_call" | custom-call | tf_op jit(solution)/shard_map/feed_forward/pallas_call | solution.py:651
  192.0 89.7 %backward.1 = (bf16[3,512,1024]{2,1,0:T(8,128)(2,1)}, bf16[3,512,1024]{2,1,0:T(8,128)(2,1)}, f32[16,8,128]{2,1,0:T(8,128)}) custom-call(s32[4]{0:T(128)} %layout.3, bf16[3,2,3,512,512]{4,3,2,1,0:T(8,128)(2,1)} %get-tuple-element.26.q_ref.k_ref.v_ref, bf16[3,2,3,512,512]{4,3,2,1,0:T(8,128)(2,1)} %get-tuple-element.26.q_ref.k_ref.v_ref, ...), custom_call_target="tpu_custom_call" | custom-call | tf_op jit(solution)/shard_map/backward/pallas_call | solution.py:953
  281.7 0.0 copy-start
  281.8 6.8 %hand_out.1 = (bf16[3,512,1024]{2,1,0:T(8,128)(2,1)}, bf16[3,512,1024]{2,1,0:T(8,128)(2,1)}) custom-call(bf16[3,512,1024]{2,1,0:T(8,128)(2,1)} %get-tuple-element.41.a_ref, bf16[3,512,1024]{2,1,0:T(8,128)(2,1)} %get-tuple-element.42.b_ref), custom_call_target="tpu_custom_call" | custom-call | tf_op jit(solution)/shard_map/hand_out/pallas_call | solution.py:985
  288.6 0.0 copy-done
  288.6 0.6 slice_bitcast_fusion
Async XLA Ops:
  281.7 6.8 %copy-start = (f32[16,8,128]{2,1,0:T(8,128)S(1)}, f32[16,8,128]{2,1,0:T(8,128)}, u32[]{:S(2)}) copy-start(f32[16,8,128]{2,1,0:T(8,128)} %get-tuple-element.45) | copy-start | bytes 196612
